TPU v7x, 32 devices: a whole 2x2x4 slice. The times are simulated.
32 devices in a mesh: groups: 2 (over x), space: 16 (over z, y, core).
Axes of the slice: x: 2, y: 2, z: 4, core: 2. Of those that a mesh axis runs over, the one named last changes fastest.
Arguments:
- slowness: float32 [512, 4096], P(('groups', 'space')), parts along dimension 0, may hold values from 0.25 to 1
- ocean: int32 [512, 4096], P(('groups', 'space')), parts along dimension 0, may hold values 0 or 1
- start_times: float32 [8, 256, 4096], P('groups', 'space'), parts along dimension 0, may hold values from 0 to 96
- source_cells: int32 [8], P('groups'), parts along dimension 0, may hold values from 0 to 1048575
- gauge_cells: int32 [4096], P(('groups', 'space')), parts along dimension 0, may hold values from 0 to 65535
- gauge_owner: int32 [4096, 1], P(('groups', 'space')), parts along dimension 0, may hold values from 0 to 15; in each aligned block of 128 rows (0 to 127, 128 to 255, ...) at most 16 rows name the same one
Outputs:
- arrival: float32 [512, 4096], P(('groups', 'space')), parts along dimension 0
- gauge_arrivals: float32 [32, 4, 256], P(('groups', 'space')), parts along dimension 0
There are 2 independent parts, one for each index of `groups`. A program takes and returns all parts, laid end to end along the dimension named above; each array names one. Nothing has to cross between parts.
Inputs may be any that keep to these rules, and one draw needn't show every extreme that they name: `gauge_owner`: among the 128 gauges of one device block, no owner is named more than 16 times, a bound that some block reaches.
All inputs are finite; a program needn't handle non-finite values. No bound on the sum of `ocean` on one device may be relied on, other than what follows from the above.
Results may differ from a plain program's by a relative error of at most 0.00016.
Values sent between devices are 32-bit elements; how exact they have to be, the bound alone decides.
A program may use at most 128 MiB of HBM per device.

v0:
```python
import jax
import jax.numpy as jnp
from jax import lax
from jax.sharding import PartitionSpec as P

SWEEPS = 8
BLOCKS = 3


far_value = 1000000.0
land_cost = 10000.0
clip_value = 48.0
root_two = 1.41421356
root_five = 2.23606798


def padded_2(shard, sides, width):
    for axis, dim in sides:
        size, length = (lax.axis_size(axis), shard.shape[dim])
        up = [(i, (i + 1) % size) for i in range(size - 1)]
        down = [(j, i) for i, j in up]
        last = lax.slice_in_dim(shard, length - width, length, axis=dim)
        leading = lax.slice_in_dim(shard, 0, width, axis=dim)
        before = lax.ppermute(last, axis, up)
        after = lax.ppermute(leading, axis, down)
        shard = jnp.concatenate([before, shard, after], axis=dim)
    return shard


def relax(padded, cost):
    height = padded.shape[1] - 4
    width = padded.shape[2] - 4

    def shifted(drow, dcol):
        return padded[:, 2 + drow : 2 + drow + height, 2 + dcol : 2 + dcol + width]

    near = jnp.minimum(
        jnp.minimum(shifted(0, 1), shifted(0, -1)), jnp.minimum(shifted(1, 0), shifted(-1, 0))
    )
    diag = jnp.minimum(
        jnp.minimum(shifted(1, 1), shifted(1, -1)), jnp.minimum(shifted(-1, 1), shifted(-1, -1))
    )
    knight = jnp.minimum(
        jnp.minimum(shifted(1, 2), shifted(1, -2)), jnp.minimum(shifted(-1, 2), shifted(-1, -2))
    )
    knight = jnp.minimum(
        knight,
        jnp.minimum(
            jnp.minimum(shifted(2, 1), shifted(2, -1)), jnp.minimum(shifted(-2, 1), shifted(-2, -1))
        ),
    )
    best = jnp.minimum(near + cost, diag + root_two * cost)
    best = jnp.minimum(best, knight + root_five * cost)
    return jnp.minimum(shifted(0, 0), best)


def fence(field, first_row, total_rows):
    rows = first_row + jnp.arange(field.shape[1], dtype=jnp.int32)
    inside = (rows >= 0) & (rows < total_rows)
    return jnp.where(inside[None, :, None], field, jnp.float32(far_value))


def on_device(slowness, ocean, start_times, source_cells, gauge_cells, gauge_owner):
    index = lax.axis_index("space")
    count = lax.axis_size("space")
    rows_dev = slowness.shape[0]
    width = slowness.shape[1]
    sources = start_times.shape[0]
    total_rows = count * rows_dev
    first_row = index * rows_dev
    cost = jnp.where(ocean == 1, slowness, jnp.float32(land_cost))
    flat = first_row * width + jnp.arange(rows_dev * width, dtype=jnp.int32).reshape(
        rows_dev, width
    )
    times = jnp.where(flat[None] == source_cells[:, None, None], jnp.float32(0.0), start_times)

    def sweep(step, field):
        padded = padded_2(field, (("space", 1),), 2)
        padded = fence(padded, first_row - 2, total_rows)
        return relax(jnp.pad(padded, ((0, 0), (0, 0), (2, 2)), constant_values=far_value), cost)

    times = lax.fori_loop(0, BLOCKS * SWEEPS, sweep, times)
    each_arrival = jnp.minimum(times, jnp.float32(clip_value)) / clip_value
    arrival = jnp.min(each_arrival, axis=0)
    values = each_arrival.reshape(sources, -1)[:, gauge_cells]
    owners = gauge_owner[:, 0]
    capacity = max(2, 2 * gauge_cells.shape[0] // count)
    slots = jnp.arange(count * capacity, dtype=jnp.int32)
    onehot = (owners[:, None] == jnp.arange(count, dtype=jnp.int32)[None, :]).astype(jnp.int32)
    ranks = jnp.sum((jnp.cumsum(onehot, axis=0) - 1) * onehot, axis=1)
    target = owners * capacity + ranks
    placing = (target[:, None] == slots[None, :]).astype(jnp.float32)
    placed = jnp.dot(
        values, placing, precision=lax.Precision.HIGHEST, preferred_element_type=jnp.float32
    )
    received = lax.all_to_all(
        placed.reshape(sources, count, capacity), "space", split_axis=1, concat_axis=1, tiled=True
    )
    result = received.reshape(1, sources, count * capacity)
    return (arrival, result)


def solution(mesh):
    return jax.shard_map(
        on_device,
        mesh=mesh,
        in_specs=(
            P(("groups", "space"), None),
            P(("groups", "space"), None),
            P("groups", "space", None),
            P("groups"),
            P(("groups", "space")),
            P(("groups", "space"), None),
        ),
        out_specs=(P(("groups", "space"), None), P(("groups", "space"), None, None)),
        check_vma=False,
    )
```

profile of v0, /device:TPU:0, one launch (start us, length us, event | category | flops | bytes accessed | tf_op | source)
XLA Modules:
  0.0 370.6 jit_solution(18091390072638009376)
XLA Ops:
  2.8 320.1 %while.12 = (s32[]{:T(128)}, f32[4,16,4096]{2,1,0:T(8,128)S(1)}, s32[]{:T(128)}, f32[16,4096]{1,0:T(8,128)S(1)}, s32[]{:T(128)}) while((s32[]{:T(128)}, f32[4,16,4096]{2,1,0:T(8,128)S(1)}, s32[]{:T(128)}, f32[16,4096]{1,0:T(8,128)S(1)}, s32[]{:T(128)}) %tuple.36), condition=%wide.region_1.2_spmd, body=%wide.region_0.1_spmd.sunk | while | flops 6094930 | bytes 11534521 | solution.py:82
  8.6 4.0 %fusion.21 = f32[4,16,4096]{2,1,0:T(8,128)S(1)} fusion(f32[4,20,4096]{2,1,0:T(8,128)S(1)} %maximum_select_fusion.2, f32[16,4096]{1,0:T(8,128)S(1)} %get-tuple-element.99, f32[16,4096]{1,0:T(8,128)S(1)} %get-tuple-element.100, f32[16,4096]{1,0:T(8,128)S(1)} %get-tuple-element.114), kind=kLoop, calls=%fused_computation.7.clone.1 | loop fusion | flops 4980736 | bytes 6553600 | tf_op jit(solution)/shard_map/while/body/eval_jaxpr/min | solution.py:54
  13.9 6.4 %collective-permute-start.1 = (f32[4,2,4096]{2,1,0:T(2,128)S(1)}, f32[4,2,4096]{2,1,0:T(2,128)S(1)}, u32[]{:S(2)}, u32[]{:S(2)}) collective-permute-start(f32[4,2,4096]{2,1,0:T(2,128)S(1)} %get-tuple-element.98), channel_id=1, source_target_pairs={{0,1},{1,2},{2,3},{3,4},{4,5},{5,6},{6,7},{7,8},{8,9},{9,10},{10,1... | collective-permute-start | bytes 393224 | tf_op jit(solution)/shard_map/while/body/eval_jaxpr/ppermute | solution.py:24
  21.7 4.0 %fusion.21 = f32[4,16,4096]{2,1,0:T(8,128)S(1)} fusion(f32[4,20,4096]{2,1,0:T(8,128)S(1)} %maximum_select_fusion.2, f32[16,4096]{1,0:T(8,128)S(1)} %get-tuple-element.99, f32[16,4096]{1,0:T(8,128)S(1)} %get-tuple-element.100, f32[16,4096]{1,0:T(8,128)S(1)} %get-tuple-element.114), kind=kLoop, calls=%fused_computation.7.clone.1 | loop fusion | flops 4980736 | bytes 6553600 | tf_op jit(solution)/shard_map/while/body/eval_jaxpr/min | solution.py:54
  27.0 6.8 %collective-permute-start.1 = (f32[4,2,4096]{2,1,0:T(2,128)S(1)}, f32[4,2,4096]{2,1,0:T(2,128)S(1)}, u32[]{:S(2)}, u32[]{:S(2)}) collective-permute-start(f32[4,2,4096]{2,1,0:T(2,128)S(1)} %get-tuple-element.98), channel_id=1, source_target_pairs={{0,1},{1,2},{2,3},{3,4},{4,5},{5,6},{6,7},{7,8},{8,9},{9,10},{10,1... | collective-permute-start | bytes 393224 | tf_op jit(solution)/shard_map/while/body/eval_jaxpr/ppermute | solution.py:24
  35.2 4.0 %fusion.21 = f32[4,16,4096]{2,1,0:T(8,128)S(1)} fusion(f32[4,20,4096]{2,1,0:T(8,128)S(1)} %maximum_select_fusion.2, f32[16,4096]{1,0:T(8,128)S(1)} %get-tuple-element.99, f32[16,4096]{1,0:T(8,128)S(1)} %get-tuple-element.100, f32[16,4096]{1,0:T(8,128)S(1)} %get-tuple-element.114), kind=kLoop, calls=%fused_computation.7.clone.1 | loop fusion | flops 4980736 | bytes 6553600 | tf_op jit(solution)/shard_map/while/body/eval_jaxpr/min | solution.py:54
  40.6 6.8 %collective-permute-start.1 = (f32[4,2,4096]{2,1,0:T(2,128)S(1)}, f32[4,2,4096]{2,1,0:T(2,128)S(1)}, u32[]{:S(2)}, u32[]{:S(2)}) collective-permute-start(f32[4,2,4096]{2,1,0:T(2,128)S(1)} %get-tuple-element.98), channel_id=1, source_target_pairs={{0,1},{1,2},{2,3},{3,4},{4,5},{5,6},{6,7},{7,8},{8,9},{9,10},{10,1... | collective-permute-start | bytes 393224 | tf_op jit(solution)/shard_map/while/body/eval_jaxpr/ppermute | solution.py:24
  48.7 4.0 %fusion.21 = f32[4,16,4096]{2,1,0:T(8,128)S(1)} fusion(f32[4,20,4096]{2,1,0:T(8,128)S(1)} %maximum_select_fusion.2, f32[16,4096]{1,0:T(8,128)S(1)} %get-tuple-element.99, f32[16,4096]{1,0:T(8,128)S(1)} %get-tuple-element.100, f32[16,4096]{1,0:T(8,128)S(1)} %get-tuple-element.114), kind=kLoop, calls=%fused_computation.7.clone.1 | loop fusion | flops 4980736 | bytes 6553600 | tf_op jit(solution)/shard_map/while/body/eval_jaxpr/min | solution.py:54
  54.1 6.8 %collective-permute-start.1 = (f32[4,2,4096]{2,1,0:T(2,128)S(1)}, f32[4,2,4096]{2,1,0:T(2,128)S(1)}, u32[]{:S(2)}, u32[]{:S(2)}) collective-permute-start(f32[4,2,4096]{2,1,0:T(2,128)S(1)} %get-tuple-element.98), channel_id=1, source_target_pairs={{0,1},{1,2},{2,3},{3,4},{4,5},{5,6},{6,7},{7,8},{8,9},{9,10},{10,1... | collective-permute-start | bytes 393224 | tf_op jit(solution)/shard_map/while/body/eval_jaxpr/ppermute | solution.py:24
  62.2 4.0 %fusion.21 = f32[4,16,4096]{2,1,0:T(8,128)S(1)} fusion(f32[4,20,4096]{2,1,0:T(8,128)S(1)} %maximum_select_fusion.2, f32[16,4096]{1,0:T(8,128)S(1)} %get-tuple-element.99, f32[16,4096]{1,0:T(8,128)S(1)} %get-tuple-element.100, f32[16,4096]{1,0:T(8,128)S(1)} %get-tuple-element.114), kind=kLoop, calls=%fused_computation.7.clone.1 | loop fusion | flops 4980736 | bytes 6553600 | tf_op jit(solution)/shard_map/while/body/eval_jaxpr/min | solution.py:54
  67.6 6.8 %collective-permute-start.1 = (f32[4,2,4096]{2,1,0:T(2,128)S(1)}, f32[4,2,4096]{2,1,0:T(2,128)S(1)}, u32[]{:S(2)}, u32[]{:S(2)}) collective-permute-start(f32[4,2,4096]{2,1,0:T(2,128)S(1)} %get-tuple-element.98), channel_id=1, source_target_pairs={{0,1},{1,2},{2,3},{3,4},{4,5},{5,6},{6,7},{7,8},{8,9},{9,10},{10,1... | collective-permute-start | bytes 393224 | tf_op jit(solution)/shard_map/while/body/eval_jaxpr/ppermute | solution.py:24
  75.7 4.0 %fusion.21 = f32[4,16,4096]{2,1,0:T(8,128)S(1)} fusion(f32[4,20,4096]{2,1,0:T(8,128)S(1)} %maximum_select_fusion.2, f32[16,4096]{1,0:T(8,128)S(1)} %get-tuple-element.99, f32[16,4096]{1,0:T(8,128)S(1)} %get-tuple-element.100, f32[16,4096]{1,0:T(8,128)S(1)} %get-tuple-element.114), kind=kLoop, calls=%fused_computation.7.clone.1 | loop fusion | flops 4980736 | bytes 6553600 | tf_op jit(solution)/shard_map/while/body/eval_jaxpr/min | solution.py:54
  81.1 6.8 %collective-permute-start.1 = (f32[4,2,4096]{2,1,0:T(2,128)S(1)}, f32[4,2,4096]{2,1,0:T(2,128)S(1)}, u32[]{:S(2)}, u32[]{:S(2)}) collective-permute-start(f32[4,2,4096]{2,1,0:T(2,128)S(1)} %get-tuple-element.98), channel_id=1, source_target_pairs={{0,1},{1,2},{2,3},{3,4},{4,5},{5,6},{6,7},{7,8},{8,9},{9,10},{10,1... | collective-permute-start | bytes 393224 | tf_op jit(solution)/shard_map/while/body/eval_jaxpr/ppermute | solution.py:24
  89.2 4.0 %fusion.21 = f32[4,16,4096]{2,1,0:T(8,128)S(1)} fusion(f32[4,20,4096]{2,1,0:T(8,128)S(1)} %maximum_select_fusion.2, f32[16,4096]{1,0:T(8,128)S(1)} %get-tuple-element.99, f32[16,4096]{1,0:T(8,128)S(1)} %get-tuple-element.100, f32[16,4096]{1,0:T(8,128)S(1)} %get-tuple-element.114), kind=kLoop, calls=%fused_computation.7.clone.1 | loop fusion | flops 4980736 | bytes 6553600 | tf_op jit(solution)/shard_map/while/body/eval_jaxpr/min | solution.py:54
  94.6 6.8 %collective-permute-start.1 = (f32[4,2,4096]{2,1,0:T(2,128)S(1)}, f32[4,2,4096]{2,1,0:T(2,128)S(1)}, u32[]{:S(2)}, u32[]{:S(2)}) collective-permute-start(f32[4,2,4096]{2,1,0:T(2,128)S(1)} %get-tuple-element.98), channel_id=1, source_target_pairs={{0,1},{1,2},{2,3},{3,4},{4,5},{5,6},{6,7},{7,8},{8,9},{9,10},{10,1... | collective-permute-start | bytes 393224 | tf_op jit(solution)/shard_map/while/body/eval_jaxpr/ppermute | solution.py:24
  102.8 4.0 %fusion.21 = f32[4,16,4096]{2,1,0:T(8,128)S(1)} fusion(f32[4,20,4096]{2,1,0:T(8,128)S(1)} %maximum_select_fusion.2, f32[16,4096]{1,0:T(8,128)S(1)} %get-tuple-element.99, f32[16,4096]{1,0:T(8,128)S(1)} %get-tuple-element.100, f32[16,4096]{1,0:T(8,128)S(1)} %get-tuple-element.114), kind=kLoop, calls=%fused_computation.7.clone.1 | loop fusion | flops 4980736 | bytes 6553600 | tf_op jit(solution)/shard_map/while/body/eval_jaxpr/min | solution.py:54
  108.1 6.8 %collective-permute-start.1 = (f32[4,2,4096]{2,1,0:T(2,128)S(1)}, f32[4,2,4096]{2,1,0:T(2,128)S(1)}, u32[]{:S(2)}, u32[]{:S(2)}) collective-permute-start(f32[4,2,4096]{2,1,0:T(2,128)S(1)} %get-tuple-element.98), channel_id=1, source_target_pairs={{0,1},{1,2},{2,3},{3,4},{4,5},{5,6},{6,7},{7,8},{8,9},{9,10},{10,1... | collective-permute-start | bytes 393224 | tf_op jit(solution)/shard_map/while/body/eval_jaxpr/ppermute | solution.py:24
  116.3 4.0 %fusion.21 = f32[4,16,4096]{2,1,0:T(8,128)S(1)} fusion(f32[4,20,4096]{2,1,0:T(8,128)S(1)} %maximum_select_fusion.2, f32[16,4096]{1,0:T(8,128)S(1)} %get-tuple-element.99, f32[16,4096]{1,0:T(8,128)S(1)} %get-tuple-element.100, f32[16,4096]{1,0:T(8,128)S(1)} %get-tuple-element.114), kind=kLoop, calls=%fused_computation.7.clone.1 | loop fusion | flops 4980736 | bytes 6553600 | tf_op jit(solution)/shard_map/while/body/eval_jaxpr/min | solution.py:54
  121.6 6.8 %collective-permute-start.1 = (f32[4,2,4096]{2,1,0:T(2,128)S(1)}, f32[4,2,4096]{2,1,0:T(2,128)S(1)}, u32[]{:S(2)}, u32[]{:S(2)}) collective-permute-start(f32[4,2,4096]{2,1,0:T(2,128)S(1)} %get-tuple-element.98), channel_id=1, source_target_pairs={{0,1},{1,2},{2,3},{3,4},{4,5},{5,6},{6,7},{7,8},{8,9},{9,10},{10,1... | collective-permute-start | bytes 393224 | tf_op jit(solution)/shard_map/while/body/eval_jaxpr/ppermute | solution.py:24
  129.8 4.0 %fusion.21 = f32[4,16,4096]{2,1,0:T(8,128)S(1)} fusion(f32[4,20,4096]{2,1,0:T(8,128)S(1)} %maximum_select_fusion.2, f32[16,4096]{1,0:T(8,128)S(1)} %get-tuple-element.99, f32[16,4096]{1,0:T(8,128)S(1)} %get-tuple-element.100, f32[16,4096]{1,0:T(8,128)S(1)} %get-tuple-element.114), kind=kLoop, calls=%fused_computation.7.clone.1 | loop fusion | flops 4980736 | bytes 6553600 | tf_op jit(solution)/shard_map/while/body/eval_jaxpr/min | solution.py:54
  135.2 6.8 %collective-permute-start.1 = (f32[4,2,4096]{2,1,0:T(2,128)S(1)}, f32[4,2,4096]{2,1,0:T(2,128)S(1)}, u32[]{:S(2)}, u32[]{:S(2)}) collective-permute-start(f32[4,2,4096]{2,1,0:T(2,128)S(1)} %get-tuple-element.98), channel_id=1, source_target_pairs={{0,1},{1,2},{2,3},{3,4},{4,5},{5,6},{6,7},{7,8},{8,9},{9,10},{10,1... | collective-permute-start | bytes 393224 | tf_op jit(solution)/shard_map/while/body/eval_jaxpr/ppermute | solution.py:24
  143.3 4.0 %fusion.21 = f32[4,16,4096]{2,1,0:T(8,128)S(1)} fusion(f32[4,20,4096]{2,1,0:T(8,128)S(1)} %maximum_select_fusion.2, f32[16,4096]{1,0:T(8,128)S(1)} %get-tuple-element.99, f32[16,4096]{1,0:T(8,128)S(1)} %get-tuple-element.100, f32[16,4096]{1,0:T(8,128)S(1)} %get-tuple-element.114), kind=kLoop, calls=%fused_computation.7.clone.1 | loop fusion | flops 4980736 | bytes 6553600 | tf_op jit(solution)/shard_map/while/body/eval_jaxpr/min | solution.py:54
  148.7 6.8 %collective-permute-start.1 = (f32[4,2,4096]{2,1,0:T(2,128)S(1)}, f32[4,2,4096]{2,1,0:T(2,128)S(1)}, u32[]{:S(2)}, u32[]{:S(2)}) collective-permute-start(f32[4,2,4096]{2,1,0:T(2,128)S(1)} %get-tuple-element.98), channel_id=1, source_target_pairs={{0,1},{1,2},{2,3},{3,4},{4,5},{5,6},{6,7},{7,8},{8,9},{9,10},{10,1... | collective-permute-start | bytes 393224 | tf_op jit(solution)/shard_map/while/body/eval_jaxpr/ppermute | solution.py:24
  156.8 4.0 %fusion.21 = f32[4,16,4096]{2,1,0:T(8,128)S(1)} fusion(f32[4,20,4096]{2,1,0:T(8,128)S(1)} %maximum_select_fusion.2, f32[16,4096]{1,0:T(8,128)S(1)} %get-tuple-element.99, f32[16,4096]{1,0:T(8,128)S(1)} %get-tuple-element.100, f32[16,4096]{1,0:T(8,128)S(1)} %get-tuple-element.114), kind=kLoop, calls=%fused_computation.7.clone.1 | loop fusion | flops 4980736 | bytes 6553600 | tf_op jit(solution)/shard_map/while/body/eval_jaxpr/min | solution.py:54
  162.2 6.8 %collective-permute-start.1 = (f32[4,2,4096]{2,1,0:T(2,128)S(1)}, f32[4,2,4096]{2,1,0:T(2,128)S(1)}, u32[]{:S(2)}, u32[]{:S(2)}) collective-permute-start(f32[4,2,4096]{2,1,0:T(2,128)S(1)} %get-tuple-element.98), channel_id=1, source_target_pairs={{0,1},{1,2},{2,3},{3,4},{4,5},{5,6},{6,7},{7,8},{8,9},{9,10},{10,1... | collective-permute-start | bytes 393224 | tf_op jit(solution)/shard_map/while/body/eval_jaxpr/ppermute | solution.py:24
  170.3 4.0 %fusion.21 = f32[4,16,4096]{2,1,0:T(8,128)S(1)} fusion(f32[4,20,4096]{2,1,0:T(8,128)S(1)} %maximum_select_fusion.2, f32[16,4096]{1,0:T(8,128)S(1)} %get-tuple-element.99, f32[16,4096]{1,0:T(8,128)S(1)} %get-tuple-element.100, f32[16,4096]{1,0:T(8,128)S(1)} %get-tuple-element.114), kind=kLoop, calls=%fused_computation.7.clone.1 | loop fusion | flops 4980736 | bytes 6553600 | tf_op jit(solution)/shard_map/while/body/eval_jaxpr/min | solution.py:54
  175.7 6.8 %collective-permute-start.1 = (f32[4,2,4096]{2,1,0:T(2,128)S(1)}, f32[4,2,4096]{2,1,0:T(2,128)S(1)}, u32[]{:S(2)}, u32[]{:S(2)}) collective-permute-start(f32[4,2,4096]{2,1,0:T(2,128)S(1)} %get-tuple-element.98), channel_id=1, source_target_pairs={{0,1},{1,2},{2,3},{3,4},{4,5},{5,6},{6,7},{7,8},{8,9},{9,10},{10,1... | collective-permute-start | bytes 393224 | tf_op jit(solution)/shard_map/while/body/eval_jaxpr/ppermute | solution.py:24
  183.8 4.0 %fusion.21 = f32[4,16,4096]{2,1,0:T(8,128)S(1)} fusion(f32[4,20,4096]{2,1,0:T(8,128)S(1)} %maximum_select_fusion.2, f32[16,4096]{1,0:T(8,128)S(1)} %get-tuple-element.99, f32[16,4096]{1,0:T(8,128)S(1)} %get-tuple-element.100, f32[16,4096]{1,0:T(8,128)S(1)} %get-tuple-element.114), kind=kLoop, calls=%fused_computation.7.clone.1 | loop fusion | flops 4980736 | bytes 6553600 | tf_op jit(solution)/shard_map/while/body/eval_jaxpr/min | solution.py:54
  189.2 6.8 %collective-permute-start.1 = (f32[4,2,4096]{2,1,0:T(2,128)S(1)}, f32[4,2,4096]{2,1,0:T(2,128)S(1)}, u32[]{:S(2)}, u32[]{:S(2)}) collective-permute-start(f32[4,2,4096]{2,1,0:T(2,128)S(1)} %get-tuple-element.98), channel_id=1, source_target_pairs={{0,1},{1,2},{2,3},{3,4},{4,5},{5,6},{6,7},{7,8},{8,9},{9,10},{10,1... | collective-permute-start | bytes 393224 | tf_op jit(solution)/shard_map/while/body/eval_jaxpr/ppermute | solution.py:24
  202.7 6.8 %collective-permute-start.1 = (f32[4,2,4096]{2,1,0:T(2,128)S(1)}, f32[4,2,4096]{2,1,0:T(2,128)S(1)}, u32[]{:S(2)}, u32[]{:S(2)}) collective-permute-start(f32[4,2,4096]{2,1,0:T(2,128)S(1)} %get-tuple-element.98), channel_id=1, source_target_pairs={{0,1},{1,2},{2,3},{3,4},{4,5},{5,6},{6,7},{7,8},{8,9},{9,10},{10,1... | collective-permute-start | bytes 393224 | tf_op jit(solution)/shard_map/while/body/eval_jaxpr/ppermute | solution.py:24
  216.3 6.8 %collective-permute-start.1 = (f32[4,2,4096]{2,1,0:T(2,128)S(1)}, f32[4,2,4096]{2,1,0:T(2,128)S(1)}, u32[]{:S(2)}, u32[]{:S(2)}) collective-permute-start(f32[4,2,4096]{2,1,0:T(2,128)S(1)} %get-tuple-element.98), channel_id=1, source_target_pairs={{0,1},{1,2},{2,3},{3,4},{4,5},{5,6},{6,7},{7,8},{8,9},{9,10},{10,1... | collective-permute-start | bytes 393224 | tf_op jit(solution)/shard_map/while/body/eval_jaxpr/ppermute | solution.py:24
  224.4 4.0 %fusion.21 = f32[4,16,4096]{2,1,0:T(8,128)S(1)} fusion(f32[4,20,4096]{2,1,0:T(8,128)S(1)} %maximum_select_fusion.2, f32[16,4096]{1,0:T(8,128)S(1)} %get-tuple-element.99, f32[16,4096]{1,0:T(8,128)S(1)} %get-tuple-element.100, f32[16,4096]{1,0:T(8,128)S(1)} %get-tuple-element.114), kind=kLoop, calls=%fused_computation.7.clone.1 | loop fusion | flops 4980736 | bytes 6553600 | tf_op jit(solution)/shard_map/while/body/eval_jaxpr/min | solution.py:54
  229.8 6.8 %collective-permute-start.1 = (f32[4,2,4096]{2,1,0:T(2,128)S(1)}, f32[4,2,4096]{2,1,0:T(2,128)S(1)}, u32[]{:S(2)}, u32[]{:S(2)}) collective-permute-start(f32[4,2,4096]{2,1,0:T(2,128)S(1)} %get-tuple-element.98), channel_id=1, source_target_pairs={{0,1},{1,2},{2,3},{3,4},{4,5},{5,6},{6,7},{7,8},{8,9},{9,10},{10,1... | collective-permute-start | bytes 393224 | tf_op jit(solution)/shard_map/while/body/eval_jaxpr/ppermute | solution.py:24
  237.9 4.0 %fusion.21 = f32[4,16,4096]{2,1,0:T(8,128)S(1)} fusion(f32[4,20,4096]{2,1,0:T(8,128)S(1)} %maximum_select_fusion.2, f32[16,4096]{1,0:T(8,128)S(1)} %get-tuple-element.99, f32[16,4096]{1,0:T(8,128)S(1)} %get-tuple-element.100, f32[16,4096]{1,0:T(8,128)S(1)} %get-tuple-element.114), kind=kLoop, calls=%fused_computation.7.clone.1 | loop fusion | flops 4980736 | bytes 6553600 | tf_op jit(solution)/shard_map/while/body/eval_jaxpr/min | solution.py:54
  243.3 6.8 %collective-permute-start.1 = (f32[4,2,4096]{2,1,0:T(2,128)S(1)}, f32[4,2,4096]{2,1,0:T(2,128)S(1)}, u32[]{:S(2)}, u32[]{:S(2)}) collective-permute-start(f32[4,2,4096]{2,1,0:T(2,128)S(1)} %get-tuple-element.98), channel_id=1, source_target_pairs={{0,1},{1,2},{2,3},{3,4},{4,5},{5,6},{6,7},{7,8},{8,9},{9,10},{10,1... | collective-permute-start | bytes 393224 | tf_op jit(solution)/shard_map/while/body/eval_jaxpr/ppermute | solution.py:24
  251.4 4.0 %fusion.21 = f32[4,16,4096]{2,1,0:T(8,128)S(1)} fusion(f32[4,20,4096]{2,1,0:T(8,128)S(1)} %maximum_select_fusion.2, f32[16,4096]{1,0:T(8,128)S(1)} %get-tuple-element.99, f32[16,4096]{1,0:T(8,128)S(1)} %get-tuple-element.100, f32[16,4096]{1,0:T(8,128)S(1)} %get-tuple-element.114), kind=kLoop, calls=%fused_computation.7.clone.1 | loop fusion | flops 4980736 | bytes 6553600 | tf_op jit(solution)/shard_map/while/body/eval_jaxpr/min | solution.py:54
  256.8 6.8 %collective-permute-start.1 = (f32[4,2,4096]{2,1,0:T(2,128)S(1)}, f32[4,2,4096]{2,1,0:T(2,128)S(1)}, u32[]{:S(2)}, u32[]{:S(2)}) collective-permute-start(f32[4,2,4096]{2,1,0:T(2,128)S(1)} %get-tuple-element.98), channel_id=1, source_target_pairs={{0,1},{1,2},{2,3},{3,4},{4,5},{5,6},{6,7},{7,8},{8,9},{9,10},{10,1... | collective-permute-start | bytes 393224 | tf_op jit(solution)/shard_map/while/body/eval_jaxpr/ppermute | solution.py:24
  264.9 4.0 %fusion.21 = f32[4,16,4096]{2,1,0:T(8,128)S(1)} fusion(f32[4,20,4096]{2,1,0:T(8,128)S(1)} %maximum_select_fusion.2, f32[16,4096]{1,0:T(8,128)S(1)} %get-tuple-element.99, f32[16,4096]{1,0:T(8,128)S(1)} %get-tuple-element.100, f32[16,4096]{1,0:T(8,128)S(1)} %get-tuple-element.114), kind=kLoop, calls=%fused_computation.7.clone.1 | loop fusion | flops 4980736 | bytes 6553600 | tf_op jit(solution)/shard_map/while/body/eval_jaxpr/min | solution.py:54
  270.3 6.8 %collective-permute-start.1 = (f32[4,2,4096]{2,1,0:T(2,128)S(1)}, f32[4,2,4096]{2,1,0:T(2,128)S(1)}, u32[]{:S(2)}, u32[]{:S(2)}) collective-permute-start(f32[4,2,4096]{2,1,0:T(2,128)S(1)} %get-tuple-element.98), channel_id=1, source_target_pairs={{0,1},{1,2},{2,3},{3,4},{4,5},{5,6},{6,7},{7,8},{8,9},{9,10},{10,1... | collective-permute-start | bytes 393224 | tf_op jit(solution)/shard_map/while/body/eval_jaxpr/ppermute | solution.py:24
  278.4 4.0 %fusion.21 = f32[4,16,4096]{2,1,0:T(8,128)S(1)} fusion(f32[4,20,4096]{2,1,0:T(8,128)S(1)} %maximum_select_fusion.2, f32[16,4096]{1,0:T(8,128)S(1)} %get-tuple-element.99, f32[16,4096]{1,0:T(8,128)S(1)} %get-tuple-element.100, f32[16,4096]{1,0:T(8,128)S(1)} %get-tuple-element.114), kind=kLoop, calls=%fused_computation.7.clone.1 | loop fusion | flops 4980736 | bytes 6553600 | tf_op jit(solution)/shard_map/while/body/eval_jaxpr/min | solution.py:54
  283.8 6.8 %collective-permute-start.1 = (f32[4,2,4096]{2,1,0:T(2,128)S(1)}, f32[4,2,4096]{2,1,0:T(2,128)S(1)}, u32[]{:S(2)}, u32[]{:S(2)}) collective-permute-start(f32[4,2,4096]{2,1,0:T(2,128)S(1)} %get-tuple-element.98), channel_id=1, source_target_pairs={{0,1},{1,2},{2,3},{3,4},{4,5},{5,6},{6,7},{7,8},{8,9},{9,10},{10,1... | collective-permute-start | bytes 393224 | tf_op jit(solution)/shard_map/while/body/eval_jaxpr/ppermute | solution.py:24
  297.3 6.8 %collective-permute-start.1 = (f32[4,2,4096]{2,1,0:T(2,128)S(1)}, f32[4,2,4096]{2,1,0:T(2,128)S(1)}, u32[]{:S(2)}, u32[]{:S(2)}) collective-permute-start(f32[4,2,4096]{2,1,0:T(2,128)S(1)} %get-tuple-element.98), channel_id=1, source_target_pairs={{0,1},{1,2},{2,3},{3,4},{4,5},{5,6},{6,7},{7,8},{8,9},{9,10},{10,1... | collective-permute-start | bytes 393224 | tf_op jit(solution)/shard_map/while/body/eval_jaxpr/ppermute | solution.py:24
  305.5 4.0 %fusion.21 = f32[4,16,4096]{2,1,0:T(8,128)S(1)} fusion(f32[4,20,4096]{2,1,0:T(8,128)S(1)} %maximum_select_fusion.2, f32[16,4096]{1,0:T(8,128)S(1)} %get-tuple-element.99, f32[16,4096]{1,0:T(8,128)S(1)} %get-tuple-element.100, f32[16,4096]{1,0:T(8,128)S(1)} %get-tuple-element.114), kind=kLoop, calls=%fused_computation.7.clone.1 | loop fusion | flops 4980736 | bytes 6553600 | tf_op jit(solution)/shard_map/while/body/eval_jaxpr/min | solution.py:54
  310.9 6.8 %collective-permute-start.1 = (f32[4,2,4096]{2,1,0:T(2,128)S(1)}, f32[4,2,4096]{2,1,0:T(2,128)S(1)}, u32[]{:S(2)}, u32[]{:S(2)}) collective-permute-start(f32[4,2,4096]{2,1,0:T(2,128)S(1)} %get-tuple-element.98), channel_id=1, source_target_pairs={{0,1},{1,2},{2,3},{3,4},{4,5},{5,6},{6,7},{7,8},{8,9},{9,10},{10,1... | collective-permute-start | bytes 393224 | tf_op jit(solution)/shard_map/while/body/eval_jaxpr/ppermute | solution.py:24
  319.0 4.0 %fusion.21 = f32[4,16,4096]{2,1,0:T(8,128)S(1)} fusion(f32[4,20,4096]{2,1,0:T(8,128)S(1)} %maximum_select_fusion.2, f32[16,4096]{1,0:T(8,128)S(1)} %get-tuple-element.99, f32[16,4096]{1,0:T(8,128)S(1)} %get-tuple-element.100, f32[16,4096]{1,0:T(8,128)S(1)} %get-tuple-element.114), kind=kLoop, calls=%fused_computation.7.clone.1 | loop fusion | flops 4980736 | bytes 6553600 | tf_op jit(solution)/shard_map/while/body/eval_jaxpr/min | solution.py:54
  323.8 16.2 %copy.11 = f32[4,16,4096]{0,2,1:T(8,128)} copy(f32[4,16,4096]{2,1,0:T(8,128)S(1)} %get-tuple-element.66) | data formatting | bytes 2097152 | tf_op jit(solution)/shard_map/div | solution.py:83
  340.5 11.2 %gather_fusion = f32[128,4]{1,0:T(8,128)S(1)} fusion(f32[4,65536]{0,1:T(8,128)} %bitcast.9, s32[1024]{0:T(1024)S(1)} %pad_clamp_fusion), kind=kCustom, calls=%fused_computation | custom fusion | bytes 4608 | tf_op jit(solution)/shard_map/gather | solution.py:85
  352.1 17.9 %all_to_all.5 = f32[4,16,16]{2,0,1:T(4,128)S(1)} all-to-all(f32[4,16,16]{2,0,1:T(4,128)S(1)} %copy.12), channel_id=1, replica_groups=mesh['groups'=2,'space'=16] {'space'}, dimensions={1} | all-to-all | bytes 8192 | tf_op jit(solution)/shard_map/all_to_all | solution.py:96
  (193 shorter events, 82.6 us)
Async XLA Ops:
  2.9 4.4 %collective-permute-start = (f32[4,2,4096]{2,1,0:T(2,128)S(1)}, f32[4,2,4096]{2,1,0:T(2,128)S(1)}, u32[]{:S(2)}, u32[]{:S(2)}) collective-permute-start(f32[4,2,4096]{2,1,0:T(2,128)S(1)} %get-tuple-element.97), channel_id=1, source_target_pairs={{1,0},{2,1},{3,2},{4,3},{5,4},{6,5},{7,6},{8,7},{9,8},{10,9},{11,1... | collective-permute-start | bytes 393224 | tf_op jit(solution)/shard_map/while/body/eval_jaxpr/ppermute | solution.py:25
  4.2 4.0 %collective-permute-start.1 = (f32[4,2,4096]{2,1,0:T(2,128)S(1)}, f32[4,2,4096]{2,1,0:T(2,128)S(1)}, u32[]{:S(2)}, u32[]{:S(2)}) collective-permute-start(f32[4,2,4096]{2,1,0:T(2,128)S(1)} %get-tuple-element.98), channel_id=1, source_target_pairs={{0,1},{1,2},{2,3},{3,4},{4,5},{5,6},{6,7},{7,8},{8,9},{9,10},{10,1... | collective-permute-start | bytes 393224 | tf_op jit(solution)/shard_map/while/body/eval_jaxpr/ppermute | solution.py:24
  12.6 7.8 %collective-permute-start = (f32[4,2,4096]{2,1,0:T(2,128)S(1)}, f32[4,2,4096]{2,1,0:T(2,128)S(1)}, u32[]{:S(2)}, u32[]{:S(2)}) collective-permute-start(f32[4,2,4096]{2,1,0:T(2,128)S(1)} %get-tuple-element.97), channel_id=1, source_target_pairs={{1,0},{2,1},{3,2},{4,3},{5,4},{6,5},{7,6},{8,7},{9,8},{10,9},{11,1... | collective-permute-start | bytes 393224 | tf_op jit(solution)/shard_map/while/body/eval_jaxpr/ppermute | solution.py:25
  13.9 7.4 %collective-permute-start.1 = (f32[4,2,4096]{2,1,0:T(2,128)S(1)}, f32[4,2,4096]{2,1,0:T(2,128)S(1)}, u32[]{:S(2)}, u32[]{:S(2)}) collective-permute-start(f32[4,2,4096]{2,1,0:T(2,128)S(1)} %get-tuple-element.98), channel_id=1, source_target_pairs={{0,1},{1,2},{2,3},{3,4},{4,5},{5,6},{6,7},{7,8},{8,9},{9,10},{10,1... | collective-permute-start | bytes 393224 | tf_op jit(solution)/shard_map/while/body/eval_jaxpr/ppermute | solution.py:24
  25.7 8.2 %collective-permute-start = (f32[4,2,4096]{2,1,0:T(2,128)S(1)}, f32[4,2,4096]{2,1,0:T(2,128)S(1)}, u32[]{:S(2)}, u32[]{:S(2)}) collective-permute-start(f32[4,2,4096]{2,1,0:T(2,128)S(1)} %get-tuple-element.97), channel_id=1, source_target_pairs={{1,0},{2,1},{3,2},{4,3},{5,4},{6,5},{7,6},{8,7},{9,8},{10,9},{11,1... | collective-permute-start | bytes 393224 | tf_op jit(solution)/shard_map/while/body/eval_jaxpr/ppermute | solution.py:25
  27.0 7.8 %collective-permute-start.1 = (f32[4,2,4096]{2,1,0:T(2,128)S(1)}, f32[4,2,4096]{2,1,0:T(2,128)S(1)}, u32[]{:S(2)}, u32[]{:S(2)}) collective-permute-start(f32[4,2,4096]{2,1,0:T(2,128)S(1)} %get-tuple-element.98), channel_id=1, source_target_pairs={{0,1},{1,2},{2,3},{3,4},{4,5},{5,6},{6,7},{7,8},{8,9},{9,10},{10,1... | collective-permute-start | bytes 393224 | tf_op jit(solution)/shard_map/while/body/eval_jaxpr/ppermute | solution.py:24
  39.3 8.2 %collective-permute-start = (f32[4,2,4096]{2,1,0:T(2,128)S(1)}, f32[4,2,4096]{2,1,0:T(2,128)S(1)}, u32[]{:S(2)}, u32[]{:S(2)}) collective-permute-start(f32[4,2,4096]{2,1,0:T(2,128)S(1)} %get-tuple-element.97), channel_id=1, source_target_pairs={{1,0},{2,1},{3,2},{4,3},{5,4},{6,5},{7,6},{8,7},{9,8},{10,9},{11,1... | collective-permute-start | bytes 393224 | tf_op jit(solution)/shard_map/while/body/eval_jaxpr/ppermute | solution.py:25
  40.6 7.8 %collective-permute-start.1 = (f32[4,2,4096]{2,1,0:T(2,128)S(1)}, f32[4,2,4096]{2,1,0:T(2,128)S(1)}, u32[]{:S(2)}, u32[]{:S(2)}) collective-permute-start(f32[4,2,4096]{2,1,0:T(2,128)S(1)} %get-tuple-element.98), channel_id=1, source_target_pairs={{0,1},{1,2},{2,3},{3,4},{4,5},{5,6},{6,7},{7,8},{8,9},{9,10},{10,1... | collective-permute-start | bytes 393224 | tf_op jit(solution)/shard_map/while/body/eval_jaxpr/ppermute | solution.py:24
  52.8 8.2 %collective-permute-start = (f32[4,2,4096]{2,1,0:T(2,128)S(1)}, f32[4,2,4096]{2,1,0:T(2,128)S(1)}, u32[]{:S(2)}, u32[]{:S(2)}) collective-permute-start(f32[4,2,4096]{2,1,0:T(2,128)S(1)} %get-tuple-element.97), channel_id=1, source_target_pairs={{1,0},{2,1},{3,2},{4,3},{5,4},{6,5},{7,6},{8,7},{9,8},{10,9},{11,1... | collective-permute-start | bytes 393224 | tf_op jit(solution)/shard_map/while/body/eval_jaxpr/ppermute | solution.py:25
  54.1 7.8 %collective-permute-start.1 = (f32[4,2,4096]{2,1,0:T(2,128)S(1)}, f32[4,2,4096]{2,1,0:T(2,128)S(1)}, u32[]{:S(2)}, u32[]{:S(2)}) collective-permute-start(f32[4,2,4096]{2,1,0:T(2,128)S(1)} %get-tuple-element.98), channel_id=1, source_target_pairs={{0,1},{1,2},{2,3},{3,4},{4,5},{5,6},{6,7},{7,8},{8,9},{9,10},{10,1... | collective-permute-start | bytes 393224 | tf_op jit(solution)/shard_map/while/body/eval_jaxpr/ppermute | solution.py:24
  66.3 8.2 %collective-permute-start = (f32[4,2,4096]{2,1,0:T(2,128)S(1)}, f32[4,2,4096]{2,1,0:T(2,128)S(1)}, u32[]{:S(2)}, u32[]{:S(2)}) collective-permute-start(f32[4,2,4096]{2,1,0:T(2,128)S(1)} %get-tuple-element.97), channel_id=1, source_target_pairs={{1,0},{2,1},{3,2},{4,3},{5,4},{6,5},{7,6},{8,7},{9,8},{10,9},{11,1... | collective-permute-start | bytes 393224 | tf_op jit(solution)/shard_map/while/body/eval_jaxpr/ppermute | solution.py:25
  67.6 7.8 %collective-permute-start.1 = (f32[4,2,4096]{2,1,0:T(2,128)S(1)}, f32[4,2,4096]{2,1,0:T(2,128)S(1)}, u32[]{:S(2)}, u32[]{:S(2)}) collective-permute-start(f32[4,2,4096]{2,1,0:T(2,128)S(1)} %get-tuple-element.98), channel_id=1, source_target_pairs={{0,1},{1,2},{2,3},{3,4},{4,5},{5,6},{6,7},{7,8},{8,9},{9,10},{10,1... | collective-permute-start | bytes 393224 | tf_op jit(solution)/shard_map/while/body/eval_jaxpr/ppermute | solution.py:24
  79.8 8.2 %collective-permute-start = (f32[4,2,4096]{2,1,0:T(2,128)S(1)}, f32[4,2,4096]{2,1,0:T(2,128)S(1)}, u32[]{:S(2)}, u32[]{:S(2)}) collective-permute-start(f32[4,2,4096]{2,1,0:T(2,128)S(1)} %get-tuple-element.97), channel_id=1, source_target_pairs={{1,0},{2,1},{3,2},{4,3},{5,4},{6,5},{7,6},{8,7},{9,8},{10,9},{11,1... | collective-permute-start | bytes 393224 | tf_op jit(solution)/shard_map/while/body/eval_jaxpr/ppermute | solution.py:25
  81.1 7.8 %collective-permute-start.1 = (f32[4,2,4096]{2,1,0:T(2,128)S(1)}, f32[4,2,4096]{2,1,0:T(2,128)S(1)}, u32[]{:S(2)}, u32[]{:S(2)}) collective-permute-start(f32[4,2,4096]{2,1,0:T(2,128)S(1)} %get-tuple-element.98), channel_id=1, source_target_pairs={{0,1},{1,2},{2,3},{3,4},{4,5},{5,6},{6,7},{7,8},{8,9},{9,10},{10,1... | collective-permute-start | bytes 393224 | tf_op jit(solution)/shard_map/while/body/eval_jaxpr/ppermute | solution.py:24
  93.3 8.2 %collective-permute-start = (f32[4,2,4096]{2,1,0:T(2,128)S(1)}, f32[4,2,4096]{2,1,0:T(2,128)S(1)}, u32[]{:S(2)}, u32[]{:S(2)}) collective-permute-start(f32[4,2,4096]{2,1,0:T(2,128)S(1)} %get-tuple-element.97), channel_id=1, source_target_pairs={{1,0},{2,1},{3,2},{4,3},{5,4},{6,5},{7,6},{8,7},{9,8},{10,9},{11,1... | collective-permute-start | bytes 393224 | tf_op jit(solution)/shard_map/while/body/eval_jaxpr/ppermute | solution.py:25
  94.6 7.8 %collective-permute-start.1 = (f32[4,2,4096]{2,1,0:T(2,128)S(1)}, f32[4,2,4096]{2,1,0:T(2,128)S(1)}, u32[]{:S(2)}, u32[]{:S(2)}) collective-permute-start(f32[4,2,4096]{2,1,0:T(2,128)S(1)} %get-tuple-element.98), channel_id=1, source_target_pairs={{0,1},{1,2},{2,3},{3,4},{4,5},{5,6},{6,7},{7,8},{8,9},{9,10},{10,1... | collective-permute-start | bytes 393224 | tf_op jit(solution)/shard_map/while/body/eval_jaxpr/ppermute | solution.py:24
  106.8 8.2 %collective-permute-start = (f32[4,2,4096]{2,1,0:T(2,128)S(1)}, f32[4,2,4096]{2,1,0:T(2,128)S(1)}, u32[]{:S(2)}, u32[]{:S(2)}) collective-permute-start(f32[4,2,4096]{2,1,0:T(2,128)S(1)} %get-tuple-element.97), channel_id=1, source_target_pairs={{1,0},{2,1},{3,2},{4,3},{5,4},{6,5},{7,6},{8,7},{9,8},{10,9},{11,1... | collective-permute-start | bytes 393224 | tf_op jit(solution)/shard_map/while/body/eval_jaxpr/ppermute | solution.py:25
  108.1 7.8 %collective-permute-start.1 = (f32[4,2,4096]{2,1,0:T(2,128)S(1)}, f32[4,2,4096]{2,1,0:T(2,128)S(1)}, u32[]{:S(2)}, u32[]{:S(2)}) collective-permute-start(f32[4,2,4096]{2,1,0:T(2,128)S(1)} %get-tuple-element.98), channel_id=1, source_target_pairs={{0,1},{1,2},{2,3},{3,4},{4,5},{5,6},{6,7},{7,8},{8,9},{9,10},{10,1... | collective-permute-start | bytes 393224 | tf_op jit(solution)/shard_map/while/body/eval_jaxpr/ppermute | solution.py:24
  120.3 8.2 %collective-permute-start = (f32[4,2,4096]{2,1,0:T(2,128)S(1)}, f32[4,2,4096]{2,1,0:T(2,128)S(1)}, u32[]{:S(2)}, u32[]{:S(2)}) collective-permute-start(f32[4,2,4096]{2,1,0:T(2,128)S(1)} %get-tuple-element.97), channel_id=1, source_target_pairs={{1,0},{2,1},{3,2},{4,3},{5,4},{6,5},{7,6},{8,7},{9,8},{10,9},{11,1... | collective-permute-start | bytes 393224 | tf_op jit(solution)/shard_map/while/body/eval_jaxpr/ppermute | solution.py:25
  121.6 7.8 %collective-permute-start.1 = (f32[4,2,4096]{2,1,0:T(2,128)S(1)}, f32[4,2,4096]{2,1,0:T(2,128)S(1)}, u32[]{:S(2)}, u32[]{:S(2)}) collective-permute-start(f32[4,2,4096]{2,1,0:T(2,128)S(1)} %get-tuple-element.98), channel_id=1, source_target_pairs={{0,1},{1,2},{2,3},{3,4},{4,5},{5,6},{6,7},{7,8},{8,9},{9,10},{10,1... | collective-permute-start | bytes 393224 | tf_op jit(solution)/shard_map/while/body/eval_jaxpr/ppermute | solution.py:24
  133.9 8.2 %collective-permute-start = (f32[4,2,4096]{2,1,0:T(2,128)S(1)}, f32[4,2,4096]{2,1,0:T(2,128)S(1)}, u32[]{:S(2)}, u32[]{:S(2)}) collective-permute-start(f32[4,2,4096]{2,1,0:T(2,128)S(1)} %get-tuple-element.97), channel_id=1, source_target_pairs={{1,0},{2,1},{3,2},{4,3},{5,4},{6,5},{7,6},{8,7},{9,8},{10,9},{11,1... | collective-permute-start | bytes 393224 | tf_op jit(solution)/shard_map/while/body/eval_jaxpr/ppermute | solution.py:25
  135.2 7.8 %collective-permute-start.1 = (f32[4,2,4096]{2,1,0:T(2,128)S(1)}, f32[4,2,4096]{2,1,0:T(2,128)S(1)}, u32[]{:S(2)}, u32[]{:S(2)}) collective-permute-start(f32[4,2,4096]{2,1,0:T(2,128)S(1)} %get-tuple-element.98), channel_id=1, source_target_pairs={{0,1},{1,2},{2,3},{3,4},{4,5},{5,6},{6,7},{7,8},{8,9},{9,10},{10,1... | collective-permute-start | bytes 393224 | tf_op jit(solution)/shard_map/while/body/eval_jaxpr/ppermute | solution.py:24
  147.4 8.2 %collective-permute-start = (f32[4,2,4096]{2,1,0:T(2,128)S(1)}, f32[4,2,4096]{2,1,0:T(2,128)S(1)}, u32[]{:S(2)}, u32[]{:S(2)}) collective-permute-start(f32[4,2,4096]{2,1,0:T(2,128)S(1)} %get-tuple-element.97), channel_id=1, source_target_pairs={{1,0},{2,1},{3,2},{4,3},{5,4},{6,5},{7,6},{8,7},{9,8},{10,9},{11,1... | collective-permute-start | bytes 393224 | tf_op jit(solution)/shard_map/while/body/eval_jaxpr/ppermute | solution.py:25
  148.7 7.8 %collective-permute-start.1 = (f32[4,2,4096]{2,1,0:T(2,128)S(1)}, f32[4,2,4096]{2,1,0:T(2,128)S(1)}, u32[]{:S(2)}, u32[]{:S(2)}) collective-permute-start(f32[4,2,4096]{2,1,0:T(2,128)S(1)} %get-tuple-element.98), channel_id=1, source_target_pairs={{0,1},{1,2},{2,3},{3,4},{4,5},{5,6},{6,7},{7,8},{8,9},{9,10},{10,1... | collective-permute-start | bytes 393224 | tf_op jit(solution)/shard_map/while/body/eval_jaxpr/ppermute | solution.py:24
  160.9 8.2 %collective-permute-start = (f32[4,2,4096]{2,1,0:T(2,128)S(1)}, f32[4,2,4096]{2,1,0:T(2,128)S(1)}, u32[]{:S(2)}, u32[]{:S(2)}) collective-permute-start(f32[4,2,4096]{2,1,0:T(2,128)S(1)} %get-tuple-element.97), channel_id=1, source_target_pairs={{1,0},{2,1},{3,2},{4,3},{5,4},{6,5},{7,6},{8,7},{9,8},{10,9},{11,1... | collective-permute-start | bytes 393224 | tf_op jit(solution)/shard_map/while/body/eval_jaxpr/ppermute | solution.py:25
  162.2 7.8 %collective-permute-start.1 = (f32[4,2,4096]{2,1,0:T(2,128)S(1)}, f32[4,2,4096]{2,1,0:T(2,128)S(1)}, u32[]{:S(2)}, u32[]{:S(2)}) collective-permute-start(f32[4,2,4096]{2,1,0:T(2,128)S(1)} %get-tuple-element.98), channel_id=1, source_target_pairs={{0,1},{1,2},{2,3},{3,4},{4,5},{5,6},{6,7},{7,8},{8,9},{9,10},{10,1... | collective-permute-start | bytes 393224 | tf_op jit(solution)/shard_map/while/body/eval_jaxpr/ppermute | solution.py:24
  174.4 8.2 %collective-permute-start = (f32[4,2,4096]{2,1,0:T(2,128)S(1)}, f32[4,2,4096]{2,1,0:T(2,128)S(1)}, u32[]{:S(2)}, u32[]{:S(2)}) collective-permute-start(f32[4,2,4096]{2,1,0:T(2,128)S(1)} %get-tuple-element.97), channel_id=1, source_target_pairs={{1,0},{2,1},{3,2},{4,3},{5,4},{6,5},{7,6},{8,7},{9,8},{10,9},{11,1... | collective-permute-start | bytes 393224 | tf_op jit(solution)/shard_map/while/body/eval_jaxpr/ppermute | solution.py:25
  175.7 7.8 %collective-permute-start.1 = (f32[4,2,4096]{2,1,0:T(2,128)S(1)}, f32[4,2,4096]{2,1,0:T(2,128)S(1)}, u32[]{:S(2)}, u32[]{:S(2)}) collective-permute-start(f32[4,2,4096]{2,1,0:T(2,128)S(1)} %get-tuple-element.98), channel_id=1, source_target_pairs={{0,1},{1,2},{2,3},{3,4},{4,5},{5,6},{6,7},{7,8},{8,9},{9,10},{10,1... | collective-permute-start | bytes 393224 | tf_op jit(solution)/shard_map/while/body/eval_jaxpr/ppermute | solution.py:24
  187.9 8.2 %collective-permute-start = (f32[4,2,4096]{2,1,0:T(2,128)S(1)}, f32[4,2,4096]{2,1,0:T(2,128)S(1)}, u32[]{:S(2)}, u32[]{:S(2)}) collective-permute-start(f32[4,2,4096]{2,1,0:T(2,128)S(1)} %get-tuple-element.97), channel_id=1, source_target_pairs={{1,0},{2,1},{3,2},{4,3},{5,4},{6,5},{7,6},{8,7},{9,8},{10,9},{11,1... | collective-permute-start | bytes 393224 | tf_op jit(solution)/shard_map/while/body/eval_jaxpr/ppermute | solution.py:25
  189.2 7.8 %collective-permute-start.1 = (f32[4,2,4096]{2,1,0:T(2,128)S(1)}, f32[4,2,4096]{2,1,0:T(2,128)S(1)}, u32[]{:S(2)}, u32[]{:S(2)}) collective-permute-start(f32[4,2,4096]{2,1,0:T(2,128)S(1)} %get-tuple-element.98), channel_id=1, source_target_pairs={{0,1},{1,2},{2,3},{3,4},{4,5},{5,6},{6,7},{7,8},{8,9},{9,10},{10,1... | collective-permute-start | bytes 393224 | tf_op jit(solution)/shard_map/while/body/eval_jaxpr/ppermute | solution.py:24
  201.4 8.2 %collective-permute-start = (f32[4,2,4096]{2,1,0:T(2,128)S(1)}, f32[4,2,4096]{2,1,0:T(2,128)S(1)}, u32[]{:S(2)}, u32[]{:S(2)}) collective-permute-start(f32[4,2,4096]{2,1,0:T(2,128)S(1)} %get-tuple-element.97), channel_id=1, source_target_pairs={{1,0},{2,1},{3,2},{4,3},{5,4},{6,5},{7,6},{8,7},{9,8},{10,9},{11,1... | collective-permute-start | bytes 393224 | tf_op jit(solution)/shard_map/while/body/eval_jaxpr/ppermute | solution.py:25
  202.7 7.8 %collective-permute-start.1 = (f32[4,2,4096]{2,1,0:T(2,128)S(1)}, f32[4,2,4096]{2,1,0:T(2,128)S(1)}, u32[]{:S(2)}, u32[]{:S(2)}) collective-permute-start(f32[4,2,4096]{2,1,0:T(2,128)S(1)} %get-tuple-element.98), channel_id=1, source_target_pairs={{0,1},{1,2},{2,3},{3,4},{4,5},{5,6},{6,7},{7,8},{8,9},{9,10},{10,1... | collective-permute-start | bytes 393224 | tf_op jit(solution)/shard_map/while/body/eval_jaxpr/ppermute | solution.py:24
  215.0 8.2 %collective-permute-start = (f32[4,2,4096]{2,1,0:T(2,128)S(1)}, f32[4,2,4096]{2,1,0:T(2,128)S(1)}, u32[]{:S(2)}, u32[]{:S(2)}) collective-permute-start(f32[4,2,4096]{2,1,0:T(2,128)S(1)} %get-tuple-element.97), channel_id=1, source_target_pairs={{1,0},{2,1},{3,2},{4,3},{5,4},{6,5},{7,6},{8,7},{9,8},{10,9},{11,1... | collective-permute-start | bytes 393224 | tf_op jit(solution)/shard_map/while/body/eval_jaxpr/ppermute | solution.py:25
  216.3 7.8 %collective-permute-start.1 = (f32[4,2,4096]{2,1,0:T(2,128)S(1)}, f32[4,2,4096]{2,1,0:T(2,128)S(1)}, u32[]{:S(2)}, u32[]{:S(2)}) collective-permute-start(f32[4,2,4096]{2,1,0:T(2,128)S(1)} %get-tuple-element.98), channel_id=1, source_target_pairs={{0,1},{1,2},{2,3},{3,4},{4,5},{5,6},{6,7},{7,8},{8,9},{9,10},{10,1... | collective-permute-start | bytes 393224 | tf_op jit(solution)/shard_map/while/body/eval_jaxpr/ppermute | solution.py:24
  228.5 8.2 %collective-permute-start = (f32[4,2,4096]{2,1,0:T(2,128)S(1)}, f32[4,2,4096]{2,1,0:T(2,128)S(1)}, u32[]{:S(2)}, u32[]{:S(2)}) collective-permute-start(f32[4,2,4096]{2,1,0:T(2,128)S(1)} %get-tuple-element.97), channel_id=1, source_target_pairs={{1,0},{2,1},{3,2},{4,3},{5,4},{6,5},{7,6},{8,7},{9,8},{10,9},{11,1... | collective-permute-start | bytes 393224 | tf_op jit(solution)/shard_map/while/body/eval_jaxpr/ppermute | solution.py:25
  229.8 7.8 %collective-permute-start.1 = (f32[4,2,4096]{2,1,0:T(2,128)S(1)}, f32[4,2,4096]{2,1,0:T(2,128)S(1)}, u32[]{:S(2)}, u32[]{:S(2)}) collective-permute-start(f32[4,2,4096]{2,1,0:T(2,128)S(1)} %get-tuple-element.98), channel_id=1, source_target_pairs={{0,1},{1,2},{2,3},{3,4},{4,5},{5,6},{6,7},{7,8},{8,9},{9,10},{10,1... | collective-permute-start | bytes 393224 | tf_op jit(solution)/shard_map/while/body/eval_jaxpr/ppermute | solution.py:24
  242.0 8.2 %collective-permute-start = (f32[4,2,4096]{2,1,0:T(2,128)S(1)}, f32[4,2,4096]{2,1,0:T(2,128)S(1)}, u32[]{:S(2)}, u32[]{:S(2)}) collective-permute-start(f32[4,2,4096]{2,1,0:T(2,128)S(1)} %get-tuple-element.97), channel_id=1, source_target_pairs={{1,0},{2,1},{3,2},{4,3},{5,4},{6,5},{7,6},{8,7},{9,8},{10,9},{11,1... | collective-permute-start | bytes 393224 | tf_op jit(solution)/shard_map/while/body/eval_jaxpr/ppermute | solution.py:25
  243.3 7.8 %collective-permute-start.1 = (f32[4,2,4096]{2,1,0:T(2,128)S(1)}, f32[4,2,4096]{2,1,0:T(2,128)S(1)}, u32[]{:S(2)}, u32[]{:S(2)}) collective-permute-start(f32[4,2,4096]{2,1,0:T(2,128)S(1)} %get-tuple-element.98), channel_id=1, source_target_pairs={{0,1},{1,2},{2,3},{3,4},{4,5},{5,6},{6,7},{7,8},{8,9},{9,10},{10,1... | collective-permute-start | bytes 393224 | tf_op jit(solution)/shard_map/while/body/eval_jaxpr/ppermute | solution.py:24
  255.5 8.2 %collective-permute-start = (f32[4,2,4096]{2,1,0:T(2,128)S(1)}, f32[4,2,4096]{2,1,0:T(2,128)S(1)}, u32[]{:S(2)}, u32[]{:S(2)}) collective-permute-start(f32[4,2,4096]{2,1,0:T(2,128)S(1)} %get-tuple-element.97), channel_id=1, source_target_pairs={{1,0},{2,1},{3,2},{4,3},{5,4},{6,5},{7,6},{8,7},{9,8},{10,9},{11,1... | collective-permute-start | bytes 393224 | tf_op jit(solution)/shard_map/while/body/eval_jaxpr/ppermute | solution.py:25
  256.8 7.8 %collective-permute-start.1 = (f32[4,2,4096]{2,1,0:T(2,128)S(1)}, f32[4,2,4096]{2,1,0:T(2,128)S(1)}, u32[]{:S(2)}, u32[]{:S(2)}) collective-permute-start(f32[4,2,4096]{2,1,0:T(2,128)S(1)} %get-tuple-element.98), channel_id=1, source_target_pairs={{0,1},{1,2},{2,3},{3,4},{4,5},{5,6},{6,7},{7,8},{8,9},{9,10},{10,1... | collective-permute-start | bytes 393224 | tf_op jit(solution)/shard_map/while/body/eval_jaxpr/ppermute | solution.py:24
  269.0 8.2 %collective-permute-start = (f32[4,2,4096]{2,1,0:T(2,128)S(1)}, f32[4,2,4096]{2,1,0:T(2,128)S(1)}, u32[]{:S(2)}, u32[]{:S(2)}) collective-permute-start(f32[4,2,4096]{2,1,0:T(2,128)S(1)} %get-tuple-element.97), channel_id=1, source_target_pairs={{1,0},{2,1},{3,2},{4,3},{5,4},{6,5},{7,6},{8,7},{9,8},{10,9},{11,1... | collective-permute-start | bytes 393224 | tf_op jit(solution)/shard_map/while/body/eval_jaxpr/ppermute | solution.py:25
  270.3 7.8 %collective-permute-start.1 = (f32[4,2,4096]{2,1,0:T(2,128)S(1)}, f32[4,2,4096]{2,1,0:T(2,128)S(1)}, u32[]{:S(2)}, u32[]{:S(2)}) collective-permute-start(f32[4,2,4096]{2,1,0:T(2,128)S(1)} %get-tuple-element.98), channel_id=1, source_target_pairs={{0,1},{1,2},{2,3},{3,4},{4,5},{5,6},{6,7},{7,8},{8,9},{9,10},{10,1... | collective-permute-start | bytes 393224 | tf_op jit(solution)/shard_map/while/body/eval_jaxpr/ppermute | solution.py:24
  282.5 8.2 %collective-permute-start = (f32[4,2,4096]{2,1,0:T(2,128)S(1)}, f32[4,2,4096]{2,1,0:T(2,128)S(1)}, u32[]{:S(2)}, u32[]{:S(2)}) collective-permute-start(f32[4,2,4096]{2,1,0:T(2,128)S(1)} %get-tuple-element.97), channel_id=1, source_target_pairs={{1,0},{2,1},{3,2},{4,3},{5,4},{6,5},{7,6},{8,7},{9,8},{10,9},{11,1... | collective-permute-start | bytes 393224 | tf_op jit(solution)/shard_map/while/body/eval_jaxpr/ppermute | solution.py:25
  283.8 7.8 %collective-permute-start.1 = (f32[4,2,4096]{2,1,0:T(2,128)S(1)}, f32[4,2,4096]{2,1,0:T(2,128)S(1)}, u32[]{:S(2)}, u32[]{:S(2)}) collective-permute-start(f32[4,2,4096]{2,1,0:T(2,128)S(1)} %get-tuple-element.98), channel_id=1, source_target_pairs={{0,1},{1,2},{2,3},{3,4},{4,5},{5,6},{6,7},{7,8},{8,9},{9,10},{10,1... | collective-permute-start | bytes 393224 | tf_op jit(solution)/shard_map/while/body/eval_jaxpr/ppermute | solution.py:24
  296.0 8.2 %collective-permute-start = (f32[4,2,4096]{2,1,0:T(2,128)S(1)}, f32[4,2,4096]{2,1,0:T(2,128)S(1)}, u32[]{:S(2)}, u32[]{:S(2)}) collective-permute-start(f32[4,2,4096]{2,1,0:T(2,128)S(1)} %get-tuple-element.97), channel_id=1, source_target_pairs={{1,0},{2,1},{3,2},{4,3},{5,4},{6,5},{7,6},{8,7},{9,8},{10,9},{11,1... | collective-permute-start | bytes 393224 | tf_op jit(solution)/shard_map/while/body/eval_jaxpr/ppermute | solution.py:25
  297.3 7.8 %collective-permute-start.1 = (f32[4,2,4096]{2,1,0:T(2,128)S(1)}, f32[4,2,4096]{2,1,0:T(2,128)S(1)}, u32[]{:S(2)}, u32[]{:S(2)}) collective-permute-start(f32[4,2,4096]{2,1,0:T(2,128)S(1)} %get-tuple-element.98), channel_id=1, source_target_pairs={{0,1},{1,2},{2,3},{3,4},{4,5},{5,6},{6,7},{7,8},{8,9},{9,10},{10,1... | collective-permute-start | bytes 393224 | tf_op jit(solution)/shard_map/while/body/eval_jaxpr/ppermute | solution.py:24
  309.6 8.2 %collective-permute-start = (f32[4,2,4096]{2,1,0:T(2,128)S(1)}, f32[4,2,4096]{2,1,0:T(2,128)S(1)}, u32[]{:S(2)}, u32[]{:S(2)}) collective-permute-start(f32[4,2,4096]{2,1,0:T(2,128)S(1)} %get-tuple-element.97), channel_id=1, source_target_pairs={{1,0},{2,1},{3,2},{4,3},{5,4},{6,5},{7,6},{8,7},{9,8},{10,9},{11,1... | collective-permute-start | bytes 393224 | tf_op jit(solution)/shard_map/while/body/eval_jaxpr/ppermute | solution.py:25
  310.9 7.8 %collective-permute-start.1 = (f32[4,2,4096]{2,1,0:T(2,128)S(1)}, f32[4,2,4096]{2,1,0:T(2,128)S(1)}, u32[]{:S(2)}, u32[]{:S(2)}) collective-permute-start(f32[4,2,4096]{2,1,0:T(2,128)S(1)} %get-tuple-element.98), channel_id=1, source_target_pairs={{0,1},{1,2},{2,3},{3,4},{4,5},{5,6},{6,7},{7,8},{8,9},{9,10},{10,1... | collective-permute-start | bytes 393224 | tf_op jit(solution)/shard_map/while/body/eval_jaxpr/ppermute | solution.py:24
  (3 other events, 33.8 us)
where the time goes:
time: 373 us; the launch traced here: 371 us
  starting transfers between devices  191 us (51%)
  other arithmetic  107 us (29%)
  local copies, waits for them, and re-layouts  30.6 us (8%)
  waiting for transfers between devices  21.3 us (6%)
  blocking collectives  17.9 us (5%)
    ppermute x24, starting transfers between devices, padded_2(): before = lax.ppermute(last, axis, up)  160 us
    min x24, other arithmetic, relax(): return jnp.minimum(shifted(0, 0), best)  95 us
    ppermute x24, starting transfers between devices, padded_2(): after = lax.ppermute(leading, axis, down)  31 us
    ppermute x24, waiting for transfers between devices, padded_2(): before = lax.ppermute(last, axis, up)  21.3 us
    all_to_all x1, blocking collectives, on_device(): lax.all_to_all(placed.reshape(sources, count, capacity), 'space', split_a...  17.9 us
    div x1, local copies, waits for them, and re-layouts, on_device(): each_arrival = jnp.minimum(times, jnp.float32(clip_value)) / clip_value  16.2 us
    gather x1, local copies, waits for them, and re-layouts, on_device(): values = each_arrival.reshape(sources, -1)[:, gauge_cells]  11.2 us
  transfers between devices with their start and end apart: 48, of which 24 were waited for; matrix products, arithmetic and copies ran while one was open for 0% of the time, Pallas kernels for 0%

commit v1 on v0

v1 whole, which is shorter than its diff:
```python
import functools

import jax
import jax.numpy as jnp
from jax import lax
from jax.experimental import pallas as pl
from jax.experimental.pallas import tpu as pltpu
from jax.sharding import PartitionSpec as P

SWEEPS = 8
BLOCKS = 3
HALO = 2 * SWEEPS

far_value = 1000000.0
land_cost = 10000.0
clip_value = 48.0
root_two = 1.41421356
root_five = 2.23606798

LANES = 128
SUBS = 8
VMEM = pl.BlockSpec(memory_space=pltpu.VMEM)
SMEM = pl.BlockSpec(memory_space=pltpu.SMEM)
PARAMS = pltpu.CompilerParams(vmem_limit_bytes=48 * 1024 * 1024)


def pack_rows(rows, phases, flat, turned, out_ref):
    @pl.loop(0, rows)
    def _(r):
        turned[...] = flat[pl.ds(pl.multiple_of(r * LANES, LANES), LANES), :].T
        for k in range(phases):
            out_ref[r, k] = turned[pl.ds(k, SUBS, stride=phases), :]


def prepare(first_ref, cells_ref, start_ref, cost_ref, times_ref, packed_ref, flat, turned):
    sources, rows, width = start_ref.shape
    tiles = width // LANES
    phases = LANES // SUBS
    high = cost_ref.shape[0]
    rowcol = lax.broadcasted_iota(jnp.int32, (rows, LANES), 0) * width + lax.broadcasted_iota(
        jnp.int32, (rows, LANES), 1
    )
    for s in range(sources):
        offset = cells_ref[s] - first_ref[0]
        for m in range(tiles):
            piece = start_ref[s, :, m * LANES : (m + 1) * LANES]
            piece = jnp.where(rowcol == offset - m * LANES, 0.0, piece)
            flat[pl.ds(s * tiles + m, rows, stride=LANES), :] = piece
    pack_rows(rows, phases, flat, turned, times_ref)
    for m in range(tiles):
        piece = cost_ref[:, m * LANES : (m + 1) * LANES]
        for s in range(sources):
            flat[pl.ds(s * tiles + m, high, stride=LANES), :] = piece
    pack_rows(high, phases, flat, turned, packed_ref)


def edge_fixers(tiles):
    sub = lax.broadcasted_iota(jnp.int32, (SUBS, LANES), 0)
    lane = lax.broadcasted_iota(jnp.int32, (SUBS, LANES), 1)
    first = lane % tiles == 0
    last = lane % tiles == tiles - 1
    far = jnp.float32(far_value)

    def from_left(x):
        y = pltpu.roll(x, 1, 0)
        z = jnp.where(first, far, pltpu.roll(y, 1, 1))
        return jnp.where(sub == 0, z, y)

    def from_right(x):
        y = pltpu.roll(x, SUBS - 1, 0)
        z = jnp.where(last, far, pltpu.roll(y, LANES - 1, 1))
        return jnp.where(sub == SUBS - 1, z, y)

    return from_left, from_right


def relax_block(tiles, fence_ref, prev_ref, cur_ref, next_ref, cost_ref, out_ref, one, two, cost2, cost5):
    rows, phases = cur_ref.shape[0], cur_ref.shape[1]
    high = cost_ref.shape[0]
    from_left, from_right = edge_fixers(tiles)

    def store_row(buf, r, vals):
        for k in range(phases):
            buf[r, 2 + k] = vals[k]
        buf[r, 0] = from_left(vals[phases - 2])
        buf[r, 1] = from_left(vals[phases - 1])
        buf[r, phases + 2] = from_right(vals[0])
        buf[r, phases + 3] = from_right(vals[1])

    @pl.loop(0, rows)
    def _(r):
        store_row(one, HALO + r, [cur_ref[r, k] for k in range(phases)])

    @pl.loop(0, HALO)
    def _(r):
        store_row(one, r, [jnp.maximum(prev_ref[r, k], fence_ref[0]) for k in range(phases)])
        store_row(
            one, HALO + rows + r, [jnp.maximum(next_ref[r, k], fence_ref[1]) for k in range(phases)]
        )

    @pl.loop(0, high)
    def _(r):
        for k in range(phases):
            c = cost_ref[r, k]
            cost2[r, k] = c * root_two
            cost5[r, k] = c * root_five

    def sweep(src, dst, lowest):
        count = (high - 2 * lowest) // 2

        @pl.loop(0, count)
        def _(pair):
            r0 = lowest + 2 * pair
            outs = ([], [])
            total = phases + 4
            t = [[src[r0 + d, k] for k in range(total)] for d in range(-2, 4)]
            for i in range(2):
                mid = t[2 + i]
                v1 = [jnp.minimum(t[1 + i][k], t[3 + i][k]) for k in range(total)]
                v2 = [
                    jnp.minimum(t[i][k], t[4 + i][k]) if 0 < k < total - 1 else None
                    for k in range(total)
                ]
                for k in range(2, phases + 2):
                    near = jnp.minimum(v1[k], jnp.minimum(mid[k - 1], mid[k + 1]))
                    diag = jnp.minimum(v1[k - 1], v1[k + 1])
                    knight = jnp.minimum(
                        jnp.minimum(v1[k - 2], v1[k + 2]), jnp.minimum(v2[k - 1], v2[k + 1])
                    )
                    best = jnp.minimum(
                        near + cost_ref[r0 + i, k - 2], diag + cost2[r0 + i, k - 2]
                    )
                    best = jnp.minimum(best, knight + cost5[r0 + i, k - 2])
                    outs[i].append(jnp.minimum(mid[k], best))
            for i in range(2):
                store_row(dst, r0 + i, outs[i])

    @pl.loop(0, SWEEPS // 2)
    def _(step):
        sweep(one, two, 4 * step + 2)
        sweep(two, one, 4 * step + 4)

    @pl.loop(0, rows)
    def _(r):
        for k in range(phases):
            out_ref[r, k] = one[HALO + r, 2 + k]


def finish(cells_ref, times_ref, arrival_ref, gauge_ref, turned, flat):
    rows, phases = times_ref.shape[0], times_ref.shape[1]
    width = arrival_ref.shape[1]
    tiles = width // LANES

    @pl.loop(0, rows)
    def _(r):
        for k in range(phases):
            x = jnp.minimum(times_ref[r, k], clip_value) / clip_value
            shift = tiles
            while shift < LANES:
                x = jnp.minimum(x, pltpu.roll(x, shift, 1))
                shift *= 2
            turned[pl.ds(k, SUBS, stride=phases), :] = x
        flat[pl.ds(pl.multiple_of(r * tiles, tiles), tiles), :] = turned[...].T[:tiles]

    for m in range(tiles):
        arrival_ref[:, m * LANES : (m + 1) * LANES] = flat[pl.ds(m, rows, stride=tiles), :]

    @pl.loop(0, gauge_ref.shape[0])
    def _(g):
        cell = cells_ref[g]
        r = cell // width
        within = (cell % width) % LANES
        gauge_ref[pl.ds(g, 1), :] = times_ref[r, within % phases, pl.ds(within // phases, 1), :]


def on_device(slowness, ocean, start_times, source_cells, gauge_cells, gauge_owner):
    index = lax.axis_index("space")
    count = lax.axis_size("space")
    rows, width = slowness.shape
    sources = start_times.shape[0]
    gauges = gauge_cells.shape[0]
    phases = LANES // SUBS
    tiles = width // LANES
    f32 = jnp.float32
    up = [(i, i + 1) for i in range(count - 1)]
    down = [(j, i) for i, j in up]
    far = jnp.float32(far_value)
    top, bottom = index == 0, index == count - 1

    cost = jnp.where(ocean == 1, slowness, jnp.float32(land_cost))
    cost_prev = jnp.where(top, far, lax.ppermute(cost[rows - HALO :], "space", up))
    cost_next = jnp.where(bottom, far, lax.ppermute(cost[:HALO], "space", down))
    cost = jnp.concatenate([cost_prev, cost, cost_next], axis=0)
    high = rows + 2 * HALO
    fence = jnp.stack([jnp.where(top, far, 0.0), jnp.where(bottom, far, 0.0)]).astype(f32)
    first = (index * (rows * width)).astype(jnp.int32).reshape(1)

    times, packed = pl.pallas_call(
        prepare,
        out_shape=(
            jax.ShapeDtypeStruct((rows, phases, SUBS, LANES), f32),
            jax.ShapeDtypeStruct((high, phases, SUBS, LANES), f32),
        ),
        in_specs=[SMEM, SMEM, VMEM, VMEM],
        out_specs=(VMEM, VMEM),
        scratch_shapes=[
            pltpu.VMEM((high * LANES, LANES), f32),
            pltpu.VMEM((LANES, LANES), f32),
        ],
        compiler_params=PARAMS,
        name="prepare",
    )(first, source_cells, start_times, cost)

    for _ in range(BLOCKS):
        prev = lax.ppermute(times[rows - HALO :], "space", up)
        following = lax.ppermute(times[:HALO], "space", down)
        times = pl.pallas_call(
            functools.partial(relax_block, tiles),
            out_shape=jax.ShapeDtypeStruct(times.shape, f32),
            in_specs=[SMEM, VMEM, VMEM, VMEM, VMEM],
            out_specs=VMEM,
            scratch_shapes=[
                pltpu.VMEM((high, phases + 4, SUBS, LANES), f32),
                pltpu.VMEM((high, phases + 4, SUBS, LANES), f32),
                pltpu.VMEM((high, phases, SUBS, LANES), f32),
                pltpu.VMEM((high, phases, SUBS, LANES), f32),
            ],
            compiler_params=PARAMS,
            name="relax",
        )(fence, prev, times, following, packed)

    arrival, lines = pl.pallas_call(
        finish,
        out_shape=(
            jax.ShapeDtypeStruct((rows, width), f32),
            jax.ShapeDtypeStruct((gauges, LANES), f32),
        ),
        in_specs=[SMEM, VMEM],
        out_specs=(VMEM, VMEM),
        scratch_shapes=[
            pltpu.VMEM((LANES, LANES), f32),
            pltpu.VMEM((rows * tiles, LANES), f32),
        ],
        compiler_params=PARAMS,
        name="finish",
    )(gauge_cells, times)

    tile = (gauge_cells % width) // LANES
    lane = jnp.arange(LANES, dtype=jnp.int32)
    lines = jnp.where(lane[None, :] % tiles == tile[:, None], lines, 0.0)
    values = jnp.sum(lines.reshape(gauges, sources, tiles), axis=2)
    values = jnp.minimum(values, jnp.float32(clip_value)) / clip_value
    owners = gauge_owner[:, 0]
    capacity = max(2, 2 * gauges // count)
    slots = jnp.arange(count * capacity, dtype=jnp.int32)
    same = (owners[:, None] == owners[None, :]) & (
        jnp.arange(gauges)[None, :] < jnp.arange(gauges)[:, None]
    )
    ranks = jnp.sum(same.astype(jnp.int32), axis=1)
    target = owners * capacity + ranks
    placing = (target[:, None] == slots[None, :]).astype(f32)
    placed = lax.dot_general(
        values, placing, (((0,), (0,)), ((), ())),
        precision=lax.Precision.HIGHEST, preferred_element_type=f32,
    )
    received = lax.all_to_all(
        placed.reshape(sources, count, capacity), "space", split_axis=1, concat_axis=1, tiled=True
    )
    return (arrival, received.reshape(1, sources, count * capacity))


def solution(mesh):
    return jax.shard_map(
        on_device,
        mesh=mesh,
        in_specs=(
            P(("groups", "space"), None),
            P(("groups", "space"), None),
            P("groups", "space", None),
            P("groups"),
            P(("groups", "space")),
            P(("groups", "space"), None),
        ),
        out_specs=(P(("groups", "space"), None), P(("groups", "space"), None, None)),
        check_vma=False,
    )
```

time: 373 us -> 196 us (0.53)
  starting transfers between devices: 191 us -> 58.5 us
  other arithmetic: 107 us -> 1.62 us
  Pallas kernels: 0 us -> 85.1 us
  local copies, waits for them, and re-layouts: 30.6 us -> 2.54 us
  blocking collectives: 17.9 us -> 30.1 us
  waiting for transfers between devices: 21.3 us -> 16.3 us
    ppermute x48 -> x8, starting transfers between devices: 191 us -> 58.5 us  [the longest x3 50.2 us: on_device(): prev = lax.ppermute(times[rows - HALO:], 'space', up)]
    min x24 -> x0, other arithmetic: 95 us -> none  [relax(): return jnp.minimum(shifted(0, 0), best)]
    pallas_call x0 -> x5, Pallas kernels: none -> 85.1 us  [the longest x3 65.2 us: on_device(): pl.pallas_call(functools.partial(relax_block, tiles), out_shape=jax.Shape...]
    div x1 -> x0, local copies, waits for them, and re-layouts: 16.2 us -> none  [on_device(): each_arrival = jnp.minimum(times, jnp.float32(clip_value)) / clip_value]
    all_to_all x1, blocking collectives: 17.9 us -> 30.1 us  [on_device(): lax.all_to_all(placed.reshape(sources, count, capacity), 'space', split_a...]
    gather x1 -> x0, local copies, waits for them, and re-layouts: 11.2 us -> none  [on_device(): values = each_arrival.reshape(sources, -1)[:, gauge_cells]]
    select_n x26 -> x4, other arithmetic: 8.26 us -> 0.15 us  [the longest x1 0.08 us: on_device(): lines = jnp.where(lane[None, :] % tiles == tile[:, None], lines, 0.0)]
    ppermute x48 -> x8, waiting for transfers between devices: 21.3 us -> 16.3 us  [the longest x3 12.8 us: on_device(): following = lax.ppermute(times[:HALO], 'space', down)]
  transfers between devices with their start and end apart: 48 -> 8, of which waited for: 24 -> 7; matrix products, arithmetic and copies ran while one was open for 0% -> 0% of each run, Pallas kernels for 0% -> 0%
where the time goes in v1:
time: 196 us; the launch traced here: 195 us
  Pallas kernels  85.1 us (43%)
  starting transfers between devices  58.5 us (30%)
  blocking collectives  30.1 us (15%)
  waiting for transfers between devices  16.3 us (8%)
  local copies, waits for them, and re-layouts  2.54 us (1%)
    pallas_call x3, Pallas kernels, on_device(): pl.pallas_call(functools.partial(relax_block, tiles), out_shape=jax.Shape...  65.2 us
    ppermute x3, starting transfers between devices, on_device(): prev = lax.ppermute(times[rows - HALO:], 'space', up)  50.2 us
    all_to_all x1, blocking collectives, on_device(): lax.all_to_all(placed.reshape(sources, count, capacity), 'space', split_a...  30.1 us
    ppermute x3, waiting for transfers between devices, on_device(): following = lax.ppermute(times[:HALO], 'space', down)  12.8 us
    pallas_call x1, Pallas kernels, on_device(): pl.pallas_call(prepare, out_shape=(jax.ShapeDtypeStruct((rows, phases, SU...  12 us
    pallas_call x1, Pallas kernels, on_device(): pl.pallas_call(finish, out_shape=(jax.ShapeDtypeStruct((rows, width), f32...  7.86 us
  transfers between devices with their start and end apart: 8, of which 7 were waited for; matrix products, arithmetic and copies ran while one was open for 0% of the time, Pallas kernels for 0%

profile of v1, /device:TPU:0, one launch (start us, length us, event | category | flops | bytes accessed | tf_op | source)
XLA Modules:
  0.0 195.2 jit_solution(10196332663426142526)
XLA Ops:
  0.6 0.0 copy-start.1
  0.6 0.0 copy-start.2
  0.7 1.1 compare_select_fusion
  1.8 1.3 collective-permute-start.1
  3.1 3.0 %collective-permute-start = (f32[16,4096]{1,0:T(8,128)S(1)}, f32[16,4096]{1,0:T(8,128)S(1)}, u32[]{:S(2)}, u32[]{:S(2)}) collective-permute-start(f32[16,4096]{1,0:T(8,128)S(1)} %compare_select_fusion), channel_id=1, source_target_pairs={{0,1},{1,2},{2,3},{3,4},{4,5},{5,6},{6,7},{7,8},{8,9},{9,10},{10,1... | collective-permute-start | bytes 786440 | tf_op jit(solution)/shard_map/ppermute | solution.py:191
  6.2 0.0 collective-permute-done.1
  6.2 1.1 collective-permute-done
  7.3 0.1 pad_maximum_fusion.cost_ref
  7.4 0.0 copy-done.1
  7.4 0.0 copy-done.2
  7.4 12.0 %prepare.1 = (f32[16,16,8,128]{3,2,1,0:T(8,128)S(1)}, f32[48,16,8,128]{3,2,1,0:T(8,128)S(1)}) custom-call(s32[1]{0:T(128)} %bitcast.2.first_ref, s32[4]{0:T(128)S(1)} %copy-done.2, f32[4,16,4096]{2,1,0:T(8,128)S(1)} %copy-done.1, f32[48,4096]{1,0:T(8,128)S(1)} %pad_maximum_fusion.cost_ref), custom_call_target="tpu_custom_call" | custom-call | tf_op jit(solution)/shard_map/prepare/pallas_call | solution.py:198
  19.4 0.0 copy-start
  19.4 1.6 copy-done
  21.0 8.5 %collective-permute-start.2 = (f32[16,16,8,128]{3,2,1,0:T(8,128)S(1)}, f32[16,16,8,128]{3,2,1,0:T(8,128)S(1)}, u32[]{:S(2)}, u32[]{:S(2)}) collective-permute-start(f32[16,16,8,128]{3,2,1,0:T(8,128)S(1)} %get-tuple-element.6.cur_ref), channel_id=1, source_target_pairs={{0,1},{1,2},{2,3},{3,4},{4,5},{5,6},{6,7},{7,8},{8,9},{9,10},{10,1... | collective-permute-start | bytes 3145736 | tf_op jit(solution)/shard_map/ppermute | solution.py:215
  29.5 1.3 collective-permute-start.3
  30.8 0.1 pad_maximum_fusion.1.fence_ref
  30.9 0.8 collective-permute-done.2.prev_ref
  31.7 4.3 %collective-permute-done.3.next_ref = f32[16,16,8,128]{3,2,1,0:T(8,128)S(1)} collective-permute-done((f32[16,16,8,128]{3,2,1,0:T(8,128)S(1)}, f32[16,16,8,128]{3,2,1,0:T(8,128)S(1)}, u32[]{:S(2)}, u32[]{:S(2)}) %collective-permute-start.3) | collective-permute-done | bytes 1048608 | tf_op jit(solution)/shard_map/ppermute | solution.py:216
  36.0 21.7 %relax.3.cur_ref = f32[16,16,8,128]{3,2,1,0:T(8,128)S(1)} custom-call(f32[2]{0:T(128)S(1)} %pad_maximum_fusion.1.fence_ref, f32[16,16,8,128]{3,2,1,0:T(8,128)S(1)} %collective-permute-done.2.prev_ref, f32[16,16,8,128]{3,2,1,0:T(8,128)S(1)} %get-tuple-element.6.cur_ref, f32[16,16,8,128]{3,2,1,0:T(8,128)S(1)} %collective-permute-done.3.next_ref, ...), custom_call_target="tpu_custom_call" | custom-call | tf_op jit(solution)/shard_map/relax/pallas_call | solution.py:217
  57.7 0.0 copy-start.4
  57.7 0.0 copy-start.3
  57.7 20.9 %collective-permute-start.4 = (f32[16,16,8,128]{3,2,1,0:T(8,128)S(1)}, f32[16,16,8,128]{3,2,1,0:T(8,128)S(1)}, u32[]{:S(2)}, u32[]{:S(2)}) collective-permute-start(f32[16,16,8,128]{3,2,1,0:T(8,128)S(1)} %relax.3.cur_ref), channel_id=1, source_target_pairs={{0,1},{1,2},{2,3},{3,4},{4,5},{5,6},{6,7},{7,8},{8,9},{9,10},{10,1... | collective-permute-start | bytes 3145736 | tf_op jit(solution)/shard_map/ppermute | solution.py:215
  78.6 1.3 collective-permute-start.5
  79.9 0.9 collective-permute-done.4.prev_ref
  80.8 4.3 %collective-permute-done.5.next_ref = f32[16,16,8,128]{3,2,1,0:T(8,128)S(1)} collective-permute-done((f32[16,16,8,128]{3,2,1,0:T(8,128)S(1)}, f32[16,16,8,128]{3,2,1,0:T(8,128)S(1)}, u32[]{:S(2)}, u32[]{:S(2)}) %collective-permute-start.5) | collective-permute-done | bytes 1048608 | tf_op jit(solution)/shard_map/ppermute | solution.py:216
  85.1 21.7 %relax.4.cur_ref = f32[16,16,8,128]{3,2,1,0:T(8,128)S(1)} custom-call(f32[2]{0:T(128)S(1)} %pad_maximum_fusion.1.fence_ref, f32[16,16,8,128]{3,2,1,0:T(8,128)S(1)} %collective-permute-done.4.prev_ref, f32[16,16,8,128]{3,2,1,0:T(8,128)S(1)} %relax.3.cur_ref, f32[16,16,8,128]{3,2,1,0:T(8,128)S(1)} %collective-permute-done.5.next_ref, f32[48,16,8,128]{3,2,1,0:T(8,128)} %copy-done), custom_call_target="tpu_custom_call" | custom-call | tf_op jit(solution)/shard_map/relax/pallas_call | solution.py:217
  106.8 20.9 %collective-permute-start.6 = (f32[16,16,8,128]{3,2,1,0:T(8,128)S(1)}, f32[16,16,8,128]{3,2,1,0:T(8,128)S(1)}, u32[]{:S(2)}, u32[]{:S(2)}) collective-permute-start(f32[16,16,8,128]{3,2,1,0:T(8,128)S(1)} %relax.4.cur_ref), channel_id=1, source_target_pairs={{0,1},{1,2},{2,3},{3,4},{4,5},{5,6},{6,7},{7,8},{8,9},{9,10},{10,1... | collective-permute-start | bytes 3145736 | tf_op jit(solution)/shard_map/ppermute | solution.py:215
  127.7 1.3 collective-permute-start.7
  129.0 0.0 copy-done.4
  129.0 0.2 convert_reduce_fusion
  129.2 0.0 copy-done.3
  129.3 0.7 collective-permute-done.6.prev_ref
  129.9 4.3 %collective-permute-done.7.next_ref = f32[16,16,8,128]{3,2,1,0:T(8,128)S(1)} collective-permute-done((f32[16,16,8,128]{3,2,1,0:T(8,128)S(1)}, f32[16,16,8,128]{3,2,1,0:T(8,128)S(1)}, u32[]{:S(2)}, u32[]{:S(2)}) %collective-permute-start.7) | collective-permute-done | bytes 1048608 | tf_op jit(solution)/shard_map/ppermute | solution.py:216
  134.2 21.7 %relax.5.times_ref = f32[16,16,8,128]{3,2,1,0:T(8,128)S(1)} custom-call(f32[2]{0:T(128)S(1)} %pad_maximum_fusion.1.fence_ref, f32[16,16,8,128]{3,2,1,0:T(8,128)S(1)} %collective-permute-done.6.prev_ref, f32[16,16,8,128]{3,2,1,0:T(8,128)S(1)} %relax.4.cur_ref, f32[16,16,8,128]{3,2,1,0:T(8,128)S(1)} %collective-permute-done.7.next_ref, f32[48,16,8,128]{3,2,1,0:T(8,128)} %copy-done), custom_call_target="tpu_custom_call" | custom-call | tf_op jit(solution)/shard_map/relax/pallas_call | solution.py:217
  156.0 7.9 %finish.1 = (f32[16,4096]{1,0:T(8,128)}, f32[128,128]{1,0:T(8,128)S(1)}) custom-call(s32[128]{0:T(128)S(1)} %copy-done.3, f32[16,16,8,128]{3,2,1,0:T(8,128)S(1)} %relax.5.times_ref), custom_call_target="tpu_custom_call" | custom-call | tf_op jit(solution)/shard_map/finish/pallas_call | solution.py:232
  163.8 0.1 compare_select_fusion.1
  163.9 0.1 copy.14
  164.0 0.2 fusion
  164.2 0.1 reshape.36
  164.4 30.1 %all_to_all.5 = f32[4,16,16]{2,0,1:T(4,128)S(1)} all-to-all(f32[4,16,16]{2,0,1:T(4,128)S(1)} %copy.15), channel_id=1, replica_groups=mesh['groups'=2,'space'=16] {'space'}, dimensions={1} | all-to-all | bytes 8192 | tf_op jit(solution)/shard_map/all_to_all | solution.py:266
  194.5 0.7 reshape.37
  (7 shorter events, 0.1 us)
Async XLA Ops:
  0.6 6.7 %copy-start.1 = (f32[4,16,4096]{2,1,0:T(8,128)S(1)}, f32[4,16,4096]{2,1,0:T(8,128)}, u32[]{:S(2)}) copy-start(f32[4,16,4096]{2,1,0:T(8,128)} %start_ref.1) | copy-start | bytes 3145732
  0.6 6.7 %copy-start.2 = (s32[4]{0:T(128)S(1)}, s32[4]{0:T(128)}, u32[]{:S(2)}) copy-start(s32[4]{0:T(128)} %cells_ref.2) | copy-start | bytes 52
  1.8 4.4 %collective-permute-start.1 = (f32[16,4096]{1,0:T(8,128)S(1)}, f32[16,4096]{1,0:T(8,128)S(1)}, u32[]{:S(2)}, u32[]{:S(2)}) collective-permute-start(f32[16,4096]{1,0:T(8,128)S(1)} %compare_select_fusion), channel_id=1, source_target_pairs={{1,0},{2,1},{3,2},{4,3},{5,4},{6,5},{7,6},{8,7},{9,8},{10,9},{11,1... | collective-permute-start | bytes 786440 | tf_op jit(solution)/shard_map/ppermute | solution.py:192
  3.1 4.2 %collective-permute-start = (f32[16,4096]{1,0:T(8,128)S(1)}, f32[16,4096]{1,0:T(8,128)S(1)}, u32[]{:S(2)}, u32[]{:S(2)}) collective-permute-start(f32[16,4096]{1,0:T(8,128)S(1)} %compare_select_fusion), channel_id=1, source_target_pairs={{0,1},{1,2},{2,3},{3,4},{4,5},{5,6},{6,7},{7,8},{8,9},{9,10},{10,1... | collective-permute-start | bytes 786440 | tf_op jit(solution)/shard_map/ppermute | solution.py:191
  19.4 1.6 copy-start
  21.0 10.7 %collective-permute-start.2 = (f32[16,16,8,128]{3,2,1,0:T(8,128)S(1)}, f32[16,16,8,128]{3,2,1,0:T(8,128)S(1)}, u32[]{:S(2)}, u32[]{:S(2)}) collective-permute-start(f32[16,16,8,128]{3,2,1,0:T(8,128)S(1)} %get-tuple-element.6.cur_ref), channel_id=1, source_target_pairs={{0,1},{1,2},{2,3},{3,4},{4,5},{5,6},{6,7},{7,8},{8,9},{9,10},{10,1... | collective-permute-start | bytes 3145736 | tf_op jit(solution)/shard_map/ppermute | solution.py:215
  29.5 6.5 %collective-permute-start.3 = (f32[16,16,8,128]{3,2,1,0:T(8,128)S(1)}, f32[16,16,8,128]{3,2,1,0:T(8,128)S(1)}, u32[]{:S(2)}, u32[]{:S(2)}) collective-permute-start(f32[16,16,8,128]{3,2,1,0:T(8,128)S(1)} %get-tuple-element.6.cur_ref), channel_id=1, source_target_pairs={{1,0},{2,1},{3,2},{4,3},{5,4},{6,5},{7,6},{8,7},{9,8},{10,9},{11,1... | collective-permute-start | bytes 3145736 | tf_op jit(solution)/shard_map/ppermute | solution.py:216
  57.7 71.3 %copy-start.4 = (s32[128,1]{0,1:T(1,128)S(1)}, s32[128,1]{0,1:T(1,128)}, u32[]{:S(2)}) copy-start(s32[128,1]{0,1:T(1,128)} %param.11) | copy-start | bytes 1540
  57.7 71.5 %copy-start.3 = (s32[128]{0:T(128)S(1)}, s32[128]{0:T(128)}, u32[]{:S(2)}) copy-start(s32[128]{0:T(128)} %cells_ref.3) | copy-start | bytes 1540
  57.7 23.1 %collective-permute-start.4 = (f32[16,16,8,128]{3,2,1,0:T(8,128)S(1)}, f32[16,16,8,128]{3,2,1,0:T(8,128)S(1)}, u32[]{:S(2)}, u32[]{:S(2)}) collective-permute-start(f32[16,16,8,128]{3,2,1,0:T(8,128)S(1)} %relax.3.cur_ref), channel_id=1, source_target_pairs={{0,1},{1,2},{2,3},{3,4},{4,5},{5,6},{6,7},{7,8},{8,9},{9,10},{10,1... | collective-permute-start | bytes 3145736 | tf_op jit(solution)/shard_map/ppermute | solution.py:215
  78.6 6.5 %collective-permute-start.5 = (f32[16,16,8,128]{3,2,1,0:T(8,128)S(1)}, f32[16,16,8,128]{3,2,1,0:T(8,128)S(1)}, u32[]{:S(2)}, u32[]{:S(2)}) collective-permute-start(f32[16,16,8,128]{3,2,1,0:T(8,128)S(1)} %relax.3.cur_ref), channel_id=1, source_target_pairs={{1,0},{2,1},{3,2},{4,3},{5,4},{6,5},{7,6},{8,7},{9,8},{10,9},{11,1... | collective-permute-start | bytes 3145736 | tf_op jit(solution)/shard_map/ppermute | solution.py:216
  106.8 23.1 %collective-permute-start.6 = (f32[16,16,8,128]{3,2,1,0:T(8,128)S(1)}, f32[16,16,8,128]{3,2,1,0:T(8,128)S(1)}, u32[]{:S(2)}, u32[]{:S(2)}) collective-permute-start(f32[16,16,8,128]{3,2,1,0:T(8,128)S(1)} %relax.4.cur_ref), channel_id=1, source_target_pairs={{0,1},{1,2},{2,3},{3,4},{4,5},{5,6},{6,7},{7,8},{8,9},{9,10},{10,1... | collective-permute-start | bytes 3145736 | tf_op jit(solution)/shard_map/ppermute | solution.py:215
  127.7 6.5 %collective-permute-start.7 = (f32[16,16,8,128]{3,2,1,0:T(8,128)S(1)}, f32[16,16,8,128]{3,2,1,0:T(8,128)S(1)}, u32[]{:S(2)}, u32[]{:S(2)}) collective-permute-start(f32[16,16,8,128]{3,2,1,0:T(8,128)S(1)} %relax.4.cur_ref), channel_id=1, source_target_pairs={{1,0},{2,1},{3,2},{4,3},{5,4},{6,5},{7,6},{8,7},{9,8},{10,9},{11,1... | collective-permute-start | bytes 3145736 | tf_op jit(solution)/shard_map/ppermute | solution.py:216

commit v2 on v0

v2 whole, which is shorter than its diff:
```python
import functools

import jax
import jax.numpy as jnp
from jax import lax
from jax.experimental import pallas as pl
from jax.experimental.pallas import tpu as pltpu
from jax.sharding import PartitionSpec as P

SWEEPS = 8
BLOCKS = 3
HALO = 2 * SWEEPS
SLAB = 4

far_value = 1000000.0
land_cost = 10000.0
clip_value = 48.0
root_two = 1.41421356
root_five = 2.23606798

LANES = 128
SUBS = 8
GROUP = 8
VMEM = pl.BlockSpec(memory_space=pltpu.VMEM)
SMEM = pl.BlockSpec(memory_space=pltpu.SMEM)
ANY = pl.BlockSpec(memory_space=pl.ANY)
PARAMS = pltpu.CompilerParams(vmem_limit_bytes=48 * 1024 * 1024)
MESH = pl.DeviceIdType.MESH


def window_start(quarter, size):
    return quarter * size - LANES * ((quarter + 2) // 3 + quarter // 3)


def remote(src, dst, send_sem, recv_sem, device):
    return pltpu.make_async_remote_copy(
        src_ref=src,
        dst_ref=dst,
        send_sem=send_sem,
        recv_sem=recv_sem,
        device_id={"space": device},
        device_id_type=MESH,
    )


def signal(barrier, device):
    pl.semaphore_signal(barrier, inc=1, device_id={"space": device}, device_id_type=MESH)


def ends(me, count):
    slab = me // SLAB
    return slab > 0, slab < count // SLAB - 1


def greet(barrier, me, count):
    below, above = ends(me, count)

    @pl.when(below)
    def _():
        signal(barrier, me - SLAB)

    @pl.when(above)
    def _():
        signal(barrier, me + SLAB)

    return below, above


def meet(barrier, me, count, others):
    slabs = count // SLAB
    slab = me // SLAB
    below = (slab + slabs - 1) // slabs
    above = (2 * slabs - 2 - slab) // slabs
    pl.semaphore_wait(barrier, others + below + above)


def trade(me, below, above, downs, ups, send_sems, recv_sems):

    def lower(n):
        return remote(*downs[n], send_sems.at[0, n], recv_sems.at[0, n], me - SLAB)

    def upper(n):
        return remote(*ups[n], send_sems.at[1, n], recv_sems.at[1, n], me + SLAB)

    def landed(side, n, dst, device):
        remote(dst, dst, send_sems.at[side, n], recv_sems.at[side, n], device).wait_recv()

    @pl.when(below)
    def _():
        for n in range(len(downs)):
            lower(n).start()

    @pl.when(above)
    def _():
        for n in range(len(ups)):
            upper(n).start()

    @pl.when(below)
    def _():
        for n in range(len(downs)):
            lower(n).wait_send()
            landed(1, n, ups[n][1], me - SLAB)

    @pl.when(above)
    def _():
        for n in range(len(ups)):
            upper(n).wait_send()
            landed(0, n, downs[n][1], me + SLAB)


def regroup(count, start_ref, cost_ref, info_ref, t_ref, c_ref, g_ref, pt, pc, nt, nc,
            local_sems, send_sems, recv_sems, far_send, far_recv):
    me = lax.axis_index("space")
    base = me // SLAB * SLAB
    p = me % SLAB
    size = start_ref.shape[2] // SLAB
    window = t_ref.shape[3]
    barrier = pltpu.get_barrier_semaphore()
    for o in range(1, SLAB):
        signal(barrier, base + (p + o) % SLAB)
    below, above = greet(barrier, me, count)
    meet(barrier, me, count, SLAB - 1)

    def pieces(q):
        cols = pl.ds(pl.multiple_of(window_start(q, size), LANES), window)
        return (
            (start_ref.at[:, :, cols], t_ref.at[p]),
            (cost_ref.at[:, cols], c_ref.at[p]),
            (info_ref, g_ref.at[p]),
        )

    def outgoing(o):
        q = (p + o) % SLAB
        return [
            remote(src, dst, send_sems.at[o - 1, n], recv_sems.at[p, n], base + q)
            for n, (src, dst) in enumerate(pieces(q))
        ]

    local = [
        pltpu.make_async_copy(src, dst, local_sems.at[n]) for n, (src, dst) in enumerate(pieces(p))
    ]
    for o in (2, 1, 3):
        for c in outgoing(o):
            c.start()
    for c in local:
        c.start()
    for c in local:
        c.wait()
    for o in range(1, SLAB):
        q = (p + o) % SLAB
        for n, ref in enumerate((t_ref, c_ref, g_ref)):
            remote(ref.at[q], ref.at[q], send_sems.at[o - 1, n], recv_sems.at[q, n], base + q).wait_recv()
    trade(me, below, above,
          ((t_ref.at[0], nt), (c_ref.at[0], nc)),
          ((t_ref.at[SLAB - 1], pt), (c_ref.at[SLAB - 1], pc)), far_send, far_recv)
    for o in range(1, SLAB):
        for c in outgoing(o):
            c.wait_send()


def swap(count, times_ref, prev_ref, next_ref, far_send, far_recv):
    me = lax.axis_index("space")
    barrier = pltpu.get_barrier_semaphore()
    below, above = greet(barrier, me, count)
    meet(barrier, me, count, 0)
    rows = times_ref.shape[0]
    trade(me, below, above,
          ((times_ref.at[pl.ds(0, HALO)], next_ref),),
          ((times_ref.at[pl.ds(rows - HALO, HALO)], prev_ref),), far_send, far_recv)


def selection(phases, back):
    size = phases * LANES
    packed = lax.broadcasted_iota(jnp.int32, (size, size), 0 if back else 1)
    plain = lax.broadcasted_iota(jnp.int32, (size, size), 1 if back else 0)
    return jnp.where(plain == packed % LANES * phases + packed // LANES, 1.0, 0.0)


def prepare(width, first_ref, cells_ref, fence_ref, t_ref, c_ref, pt, pc, nt, nc, times_ref,
            packed_ref, choose):
    _, sources, rows, window = t_ref.shape
    half = window // 2
    phases = half // LANES
    choose[...] = selection(phases, False)
    row = lax.broadcasted_iota(jnp.int32, (rows, half), 0)
    col = lax.broadcasted_iota(jnp.int32, (rows, half), 1)
    place = row * width + col
    far = jnp.float32(far_value)

    def arrange(x):
        return jnp.dot(
            x, choose[...], precision=lax.Precision.HIGHEST, preferred_element_type=jnp.float32
        )

    def put(ref, block, h, s, y, k):
        start = (block * rows * phases + k) * SUBS + s * 2 + h
        ref[pl.ds(start, rows, stride=phases * SUBS), :] = y

    for block in range(SLAB + 2):
        outside = None
        if block in (0, SLAB + 1):
            outside = fence_ref[0 if block == 0 else 1] > 0.0
        for h in range(2):
            cols = slice(h * half, (h + 1) * half)
            xs = []
            for s in range(sources):
                if block == 0:
                    x = pt[s, :, cols]
                elif block == SLAB + 1:
                    x = nt[s, :, cols]
                else:
                    x = t_ref[block - 1, s, :, cols]
                offset = cells_ref[s] - (first_ref[0] + (block - 1) * rows * width + h * half)
                x = jnp.where(place == offset, 0.0, x)
                xs.append(x)
            if block == 0:
                c = pc[:, cols]
            elif block == SLAB + 1:
                c = nc[:, cols]
            else:
                c = c_ref[block - 1, :, cols]
            xs.append(c)
            if outside is not None:
                xs = [jnp.where(outside, far, x) for x in xs]
            y = arrange(jnp.concatenate(xs, axis=0))
            for k in range(phases):
                for s in range(sources):
                    put(times_ref, block, h, s, y[s * rows : (s + 1) * rows, k * LANES : (k + 1) * LANES], k)
                    put(packed_ref, block, h, s, y[sources * rows :, k * LANES : (k + 1) * LANES], k)


def edge_fixers():
    sub = lax.broadcasted_iota(jnp.int32, (SUBS, LANES), 0)
    lane = lax.broadcasted_iota(jnp.int32, (SUBS, LANES), 1)
    far = jnp.float32(far_value)

    def from_left(x):
        y = pltpu.roll(x, 1, 1)
        z = jnp.where(sub % 2 == 0, far, pltpu.roll(y, 1, 0))
        return jnp.where(lane == 0, z, y)

    def from_right(x):
        y = pltpu.roll(x, LANES - 1, 1)
        z = jnp.where(sub % 2 == 1, far, pltpu.roll(y, SUBS - 1, 0))
        return jnp.where(lane == LANES - 1, z, y)

    return from_left, from_right


def relax_block(fence_ref, prev_ref, cur_ref, next_ref, cost_ref, out_ref, one, two, cost2, cost5):
    rows, phases = cur_ref.shape[0], cur_ref.shape[1]
    high = cost_ref.shape[0]
    total = phases + 4
    far = jnp.float32(far_value)
    from_left, from_right = edge_fixers()

    def store_row(buf, r, vals):
        for k in range(phases):
            buf[r, 2 + k] = vals[k]
        buf[r, 0] = from_left(vals[phases - 2])
        buf[r, 1] = from_left(vals[phases - 1])
        buf[r, phases + 2] = from_right(vals[0])
        buf[r, phases + 3] = from_right(vals[1])

    @pl.loop(0, rows // 4)
    def _(g):
        for i in range(4):
            r = 4 * g + i
            store_row(one, HALO + r, [cur_ref[r, k] for k in range(phases)])

    for ref, start, n in ((prev_ref, 0, 0), (next_ref, HALO + rows, 1)):

        @pl.loop(0, HALO // 4)
        def _(g):
            for i in range(4):
                r = 4 * g + i
                vals = [jnp.where(fence_ref[n] > 0.0, far, ref[r, k]) for k in range(phases)]
                store_row(one, start + r, vals)

    @pl.loop(0, high // 4)
    def _(g):
        for i in range(4):
            for k in range(phases):
                c = cost_ref[4 * g + i, k]
                cost2[4 * g + i, k] = c * root_two
                cost5[4 * g + i, k] = c * root_five

    def sweep(src, dst, lowest):
        groups = (high - 2 * lowest + GROUP - 1) // GROUP

        def begin(group):
            return jnp.minimum(lowest + GROUP * group, high - lowest - GROUP)

        def edges(start):
            for i in range(GROUP):
                r = start + i
                dst[r, 0] = from_left(dst[r, phases])
                dst[r, 1] = from_left(dst[r, phases + 1])
                dst[r, phases + 2] = from_right(dst[r, 2])
                dst[r, phases + 3] = from_right(dst[r, 3])

        @pl.loop(0, groups)
        def _(group):
            r0 = begin(group)
            edges(begin(jnp.maximum(group - 1, 0)))
            t = {}

            def load(d):
                inner = range(1, total - 1) if d in (-2, GROUP + 1) else range(total)
                t[d] = {x: src[r0 + d, x] for x in inner}

            for d in (-2, -1, 0, 1):
                load(d)
            for i in range(GROUP):
                load(i + 2)
                r = r0 + i
                m = t[i]
                a = [jnp.minimum(t[i - 1][x], t[i + 1][x]) for x in range(total)]
                b = {x: jnp.minimum(t[i - 2][x], t[i + 2][x]) for x in range(1, total - 1)}
                for k in range(2, phases + 2):
                    near = jnp.minimum(a[k], jnp.minimum(m[k - 1], m[k + 1]))
                    diag = jnp.minimum(a[k - 1], a[k + 1])
                    knight = jnp.minimum(
                        jnp.minimum(a[k - 2], a[k + 2]), jnp.minimum(b[k - 1], b[k + 1])
                    )
                    best = jnp.minimum(near + cost_ref[r, k - 2], diag + cost2[r, k - 2])
                    best = jnp.minimum(best, knight + cost5[r, k - 2])
                    dst[r, k] = jnp.minimum(m[k], best)

        edges(begin(groups - 1))

    @pl.loop(0, SWEEPS // 2)
    def _(step):
        sweep(one, two, 4 * step + 2)
        sweep(two, one, 4 * step + 4)

    @pl.loop(0, rows)
    def _(r):
        for k in range(phases):
            out_ref[r, k] = one[HALO + r, 2 + k]


def finish(spots_ref, turns_ref, times_ref, arrival_ref, gauge_ref, least, choose):
    slab, rows, window = arrival_ref.shape
    half = window // 2
    phases = half // LANES
    choose[...] = selection(phases, True)
    steps = slab * rows * phases
    lane = lax.broadcasted_iota(jnp.int32, (SUBS, LANES), 1)

    @pl.loop(0, steps // SUBS)
    def _(group):
        for i in range(SUBS):
            row = pl.ds(pl.multiple_of((group * SUBS + i) * SUBS, SUBS), SUBS)
            x = times_ref[row, :]
            x = jnp.minimum(x, pltpu.roll(x, 2, 0))
            least[row, :] = jnp.minimum(x, pltpu.roll(x, 4, 0))

    for h in range(2):
        x = jnp.concatenate(
            [least[pl.ds(k * SUBS + h, slab * rows, stride=phases * SUBS), :] for k in range(phases)],
            axis=1,
        )
        x = jnp.minimum(x, clip_value) / clip_value
        y = jnp.dot(x, choose[...], precision=lax.Precision.HIGHEST, preferred_element_type=jnp.float32)
        for b in range(slab):
            arrival_ref[b, :, h * half : (h + 1) * half] = y[b * rows : (b + 1) * rows]

    gauges = gauge_ref.shape[2]
    for b in range(slab):
        for start in range(0, gauges, LANES):

            def step(group, acc):
                for i in range(SUBS):
                    n = group * SUBS + i
                    g = b * gauges + start + n
                    x = times_ref[pl.ds(pl.multiple_of(spots_ref[g], SUBS), SUBS), :]
                    x = pltpu.roll(x, turns_ref[g], 1)
                    acc = jnp.where(lane == n, x, acc)
                return acc

            acc = lax.fori_loop(0, LANES // SUBS, step, jnp.zeros((SUBS, LANES), jnp.float32))
            gauge_ref[b, :, start : start + LANES] = acc


def deliver(count, size, arrival_ref, send_ref, out_ref, recv_ref, send_sems, recv_sems,
            slab_send, slab_recv, local_sems):
    me = lax.axis_index("space")
    base = me // SLAB * SLAB
    p = me % SLAB
    barrier = pltpu.get_barrier_semaphore()

    @pl.loop(1, count)
    def _(step):
        signal(barrier, lax.rem(me + step, count))

    pl.semaphore_wait(barrier, count - 1)
    mine = pl.ds(pl.multiple_of(p * size - window_start(p, size), LANES), size)

    def columns(q):
        return pl.ds(pl.multiple_of(q * size, LANES), size)

    def block(o):
        q = (p + o) % SLAB
        return remote(
            arrival_ref.at[q, :, mine], out_ref.at[:, columns(p)],
            slab_send.at[o - 1], slab_recv.at[p], base + q,
        )

    def copy_to(peer):
        return remote(send_ref.at[peer], recv_ref.at[me], send_sems.at[peer], recv_sems.at[me], peer)

    for o in (2, 1, 3):
        block(o).start()

    @pl.loop(1, count)
    def _(step):
        copy_to(lax.rem(me + step, count)).start()

    own = pltpu.make_async_copy(arrival_ref.at[p, :, mine], out_ref.at[:, columns(p)], local_sems.at[0])
    kept = pltpu.make_async_copy(send_ref.at[me], recv_ref.at[me], local_sems.at[1])
    own.start()
    kept.start()
    own.wait()
    kept.wait()

    @pl.loop(1, count)
    def _(step):
        peer = lax.rem(me + step, count)
        copy_to(peer).wait_send()
        remote(send_ref.at[peer], recv_ref.at[peer], send_sems.at[peer], recv_sems.at[peer], peer).wait_recv()

    for o in range(1, SLAB):
        q = (p + o) % SLAB
        block(o).wait_send()
        remote(
            arrival_ref.at[q, :, mine], out_ref.at[:, columns(q)],
            slab_send.at[o - 1], slab_recv.at[q], base + q,
        ).wait_recv()


def on_device(slowness, ocean, start_times, source_cells, gauge_cells, gauge_owner):
    index = lax.axis_index("space")
    count = lax.axis_size("space")
    rows, width = slowness.shape
    sources = start_times.shape[0]
    gauges = gauge_cells.shape[0]
    size = width // SLAB
    window = size + 2 * LANES
    half = window // 2
    phases = half // LANES
    f32 = jnp.float32
    high = rows * SLAB + 2 * HALO
    far = jnp.float32(far_value)
    q = index % SLAB
    slab = index // SLAB
    left = window_start(q, size)

    cost = jnp.where(ocean == 1, slowness, jnp.float32(land_cost))
    info = jnp.stack([gauge_cells, gauge_owner[:, 0]])[:, None, :]
    fence = jnp.stack([jnp.where(slab == 0, 1.0, 0.0), jnp.where(slab == count // SLAB - 1, 1.0, 0.0)])
    fence = fence.astype(f32)
    first = (slab * (SLAB * rows * width) + left).astype(jnp.int32).reshape(1)
    dma = pltpu.SemaphoreType.DMA

    piece_t = jax.ShapeDtypeStruct((sources, rows, window), f32)
    piece_c = jax.ShapeDtypeStruct((rows, window), f32)
    t4, c4, g4, pt, pc, nt, nc = pl.pallas_call(
        functools.partial(regroup, count),
        out_shape=(
            jax.ShapeDtypeStruct((SLAB,) + piece_t.shape, f32),
            jax.ShapeDtypeStruct((SLAB,) + piece_c.shape, f32),
            jax.ShapeDtypeStruct((SLAB,) + info.shape, jnp.int32),
            piece_t, piece_c, piece_t, piece_c,
        ),
        in_specs=[ANY] * 3,
        out_specs=(ANY,) * 7,
        scratch_shapes=[dma((3,)), dma((SLAB - 1, 3)), dma((SLAB, 3)), dma((2, 2)), dma((2, 2))],
        compiler_params=pltpu.CompilerParams(collective_id=0, has_side_effects=True),
        name="regroup",
    )(start_times, cost, info)

    flat = jax.ShapeDtypeStruct((high * phases * SUBS, LANES), f32)
    times, packed = pl.pallas_call(
        functools.partial(prepare, width),
        out_shape=(flat, flat),
        in_specs=[SMEM] * 3 + [VMEM] * 6,
        out_specs=(VMEM, VMEM),
        scratch_shapes=[pltpu.VMEM((half, half), f32)],
        compiler_params=PARAMS,
        name="prepare",
    )(first, source_cells, fence, t4, c4, pt, pc, nt, nc)
    packed = packed.reshape(high, phases, SUBS, LANES)
    times = times.reshape(high, phases, SUBS, LANES)
    prev, times, following = times[:HALO], times[HALO : high - HALO], times[high - HALO :]

    for block in range(BLOCKS):
        if block:
            halo = jax.ShapeDtypeStruct((HALO,) + times.shape[1:], f32)
            prev, following = pl.pallas_call(
                functools.partial(swap, count),
                out_shape=(halo, halo),
                in_specs=[ANY],
                out_specs=(ANY, ANY),
                scratch_shapes=[dma((2, 1)), dma((2, 1))],
                compiler_params=pltpu.CompilerParams(collective_id=block, has_side_effects=True),
                name=f"swap_{block}",
            )(times)
        times = pl.pallas_call(
            relax_block,
            out_shape=jax.ShapeDtypeStruct(times.shape, f32),
            in_specs=[SMEM, VMEM, VMEM, VMEM, VMEM],
            out_specs=VMEM,
            scratch_shapes=[
                pltpu.VMEM((high, phases + 4, SUBS, LANES), f32),
                pltpu.VMEM((high, phases + 4, SUBS, LANES), f32),
                pltpu.VMEM((high, phases, SUBS, LANES), f32),
                pltpu.VMEM((high, phases, SUBS, LANES), f32),
            ],
            compiler_params=PARAMS,
            name="relax",
        )(fence, prev, times, following, packed)

    cells, owners = g4[:, 0, 0], g4[:, 1, 0]
    column = cells % width
    inside = column // size == q
    local = jnp.clip(column - left, 0, window - 1)
    where = local % half
    grid_row = jnp.arange(SLAB, dtype=jnp.int32)[:, None] * rows + cells // width
    spots = (grid_row * phases + where % phases) * SUBS
    turns = (jnp.arange(gauges, dtype=jnp.int32)[None, :] - where // phases) % LANES
    arrival, lines = pl.pallas_call(
        finish,
        out_shape=(
            jax.ShapeDtypeStruct((SLAB, rows, window), f32),
            jax.ShapeDtypeStruct((SLAB, SUBS, gauges), f32),
        ),
        in_specs=[SMEM, SMEM, VMEM],
        out_specs=(VMEM, VMEM),
        scratch_shapes=[
            pltpu.VMEM((SLAB * rows * phases * SUBS, LANES), f32),
            pltpu.VMEM((half, half), f32),
        ],
        compiler_params=PARAMS,
        name="finish",
    )(spots.reshape(-1), turns.reshape(-1), times.reshape(-1, LANES))

    lines = lines.reshape(SLAB, sources, 2, gauges)
    values = jnp.where((local // half == 0)[:, None, :], lines[:, :, 0], lines[:, :, 1])
    values = jnp.minimum(values, jnp.float32(clip_value)) / clip_value
    values = jnp.where(inside[:, None, :], values, 0.0)
    capacity = max(2, 2 * gauges // count)
    slots = jnp.arange(count * capacity, dtype=jnp.int32)
    same = (owners[:, :, None] == owners[:, None, :]) & (
        jnp.arange(gauges)[None, :] < jnp.arange(gauges)[:, None]
    )
    ranks = jnp.sum(same.astype(jnp.int32), axis=2)
    target = owners * capacity + ranks
    placing = (target[:, :, None] == slots[None, None, :]).astype(f32)
    placed = jnp.einsum(
        "bsg,bgt->bst", values, placing,
        precision=lax.Precision.HIGHEST, preferred_element_type=f32,
    )
    amount = SLAB * sources * capacity
    lanes = -(-amount // LANES) * LANES
    placed = placed.reshape(SLAB, sources, count, capacity).transpose(2, 0, 1, 3)
    placed = jnp.pad(placed.reshape(count, 1, amount), ((0, 0), (0, 0), (0, lanes - amount)))
    arrival, received = pl.pallas_call(
        functools.partial(deliver, count, size),
        out_shape=(jax.ShapeDtypeStruct((rows, width), f32), jax.ShapeDtypeStruct(placed.shape, f32)),
        in_specs=[VMEM, VMEM],
        out_specs=(VMEM, VMEM),
        scratch_shapes=[dma((count,)), dma((count,)), dma((SLAB - 1,)), dma((SLAB,)), dma((2,))],
        compiler_params=pltpu.CompilerParams(collective_id=BLOCKS, has_side_effects=True),
        name="deliver",
    )(arrival, placed)
    received = received[:, 0, :amount].reshape(count // SLAB, SLAB, SLAB, sources, capacity)
    received = jnp.sum(received, axis=1).transpose(2, 0, 1, 3)
    return (arrival, received.reshape(1, sources, count * capacity))


def solution(mesh):
    return jax.shard_map(
        on_device,
        mesh=mesh,
        in_specs=(
            P(("groups", "space"), None),
            P(("groups", "space"), None),
            P("groups", "space", None),
            P("groups"),
            P(("groups", "space")),
            P(("groups", "space"), None),
        ),
        out_specs=(P(("groups", "space"), None), P(("groups", "space"), None, None)),
        check_vma=False,
    )
```

time: 373 us -> 155 us (0.42)
  starting transfers between devices: 191 us -> 0 us
  Pallas kernels: 0 us -> 129 us
  other arithmetic: 107 us -> 4.25 us
  waiting for transfers between devices: 21.3 us -> 0 us
  blocking collectives: 17.9 us -> 0 us
  local copies, waits for them, and re-layouts: 30.6 us -> 20.4 us
    ppermute x48 -> x0, starting transfers between devices: 191 us -> none  [the longest x24 160 us: padded_2(): before = lax.ppermute(last, axis, up)]
    pallas_call x0 -> x9, Pallas kernels: none -> 129 us  [the longest x3 45.9 us: on_device(): pl.pallas_call(relax_block, out_shape=jax.ShapeDtypeStruct(times.shape, f...]
    min x24 -> x0, other arithmetic: 95 us -> none  [relax(): return jnp.minimum(shifted(0, 0), best)]
    ppermute x48 -> x0, waiting for transfers between devices: 21.3 us -> none  [the longest x24 21.3 us: padded_2(): before = lax.ppermute(last, axis, up)]
    unnamed x6 -> x37, local copies, waits for them, and re-layouts: 0.19 us -> 18.5 us
    all_to_all x1 -> x0, blocking collectives: 17.9 us -> none  [on_device(): lax.all_to_all(placed.reshape(sources, count, capacity), 'space', split_a...]
    div x1 -> x0, local copies, waits for them, and re-layouts: 16.2 us -> none  [on_device(): each_arrival = jnp.minimum(times, jnp.float32(clip_value)) / clip_value]
    gather x1 -> x0, local copies, waits for them, and re-layouts: 11.2 us -> none  [on_device(): values = each_arrival.reshape(sources, -1)[:, gauge_cells]]
  transfers between devices with their start and end apart: 48 -> 0, of which waited for: 24 -> 0; matrix products, arithmetic and copies ran while one was open for 0% -> 0% of each run, Pallas kernels for 0% -> 0%
where the time goes in v2:
time: 155 us
  Pallas kernels  129 us (83%)
  local copies, waits for them, and re-layouts  20.4 us (13%)
  other arithmetic  4.25 us (3%)
    pallas_call x3, Pallas kernels, on_device(): pl.pallas_call(relax_block, out_shape=jax.ShapeDtypeStruct(times.shape, f...  45.9 us
    pallas_call x1, Pallas kernels, on_device(): pl.pallas_call(functools.partial(regroup, count), out_shape=(jax.ShapeDty...  34 us
    pallas_call x2, Pallas kernels, on_device(): pl.pallas_call(functools.partial(swap, count), out_shape=(halo, halo), in...  19.7 us
    unnamed x37, local copies, waits for them, and re-layouts  18.5 us
    pallas_call x1, Pallas kernels, on_device(): pl.pallas_call(functools.partial(prepare, width), out_shape=(flat, flat),...  11.6 us
    pallas_call x1, Pallas kernels, on_device(): pl.pallas_call(functools.partial(deliver, count, size), out_shape=(jax.Sh...  9.67 us
    pallas_call x1, Pallas kernels, on_device(): pl.pallas_call(finish, out_shape=(jax.ShapeDtypeStruct((SLAB, rows, windo...  7.84 us

profile of v2, /device:TPU:0, one launch (start us, length us, event | category | flops | bytes accessed | tf_op | source)
XLA Modules:
  0.0 154.6 jit_solution(9405905677123066178)
XLA Ops:
  0.6 0.0 copy-start.16
  0.7 0.1 pad_maximum_fusion.fence_ref
  0.7 1.8 %compare_select_fusion.cost_ref = f32[16,4096]{1,0:T(8,128)} fusion(f32[16,4096]{1,0:T(8,128)} %param.6, s32[16,4096]{1,0:T(8,128)} %param.7), kind=kLoop, calls=%fused_computation.4 | loop fusion | flops 131072 | bytes 786432 | tf_op jit(solution)/shard_map/jit(_where)/select_n | solution.py:459
  2.5 1.2 pad_add_fusion
  3.7 34.0 %regroup.1 = (f32[4,4,16,1280]{3,2,1,0:T(8,128)}, f32[4,16,1280]{2,1,0:T(8,128)}, s32[4,2,1,128]{3,2,1,0:T(1,128)}, f32[4,16,1280]{2,1,0:T(8,128)}, f32[16,1280]...) custom-call(f32[4,16,4096]{2,1,0:T(8,128)} %start_ref.1, f32[16,4096]{1,0:T(8,128)} %compare_select_fusion.cost_ref, ...), custom_call_target="tpu_custom_call" | custom-call | tf_op jit(solution)/shard_map/regroup/pallas_call | solution.py:468
  37.8 0.0 copy-done.16
  37.8 0.0 copy-start.5
  37.8 1.3 copy-done.5
  39.1 0.0 copy-start.6
  39.1 1.0 copy-done.6
  40.1 1.0 copy-done.7
  41.0 1.0 copy-done.8
  42.0 0.9 copy-done.14
  42.9 0.9 copy-done.15
  43.8 11.6 %prepare.1 = (f32[3840,128]{1,0:T(8,128)S(1)}, f32[3840,128]{1,0:T(8,128)}) custom-call(s32[1]{0:T(128)} %bitcast.8.first_ref, s32[4]{0:T(128)S(1)} %copy-done.16, f32[2]{0:T(128)S(1)} %pad_maximum_fusion.fence_ref, f32[4,4,16,1280]{3,2,1,0:T(8,128)S(1)} %copy-done.5, f32[4,16,1280]{2,1,0:T(8,128)S(1)} %copy-done.6, f32[4,16,1280]{2,1,0:T(8,128)S(1)} %copy-done.7, ...), custom_call_target="tpu_custom_call" | custom-call | tf_op jit(solution)/shard_map/prepare/pallas_call | solution.py:484
  55.4 0.1 slice.33
  55.6 1.4 copy-done
  57.0 15.3 %relax.3.times_ref.cur_ref = f32[64,5,8,128]{3,2,1,0:T(8,128)S(1)} custom-call(f32[2]{0:T(128)S(1)} %pad_maximum_fusion.fence_ref, f32[16,5,8,128]{3,2,1,0:T(8,128)S(1)} %bitcast.39, f32[64,5,8,128]{3,2,1,0:T(8,128)S(1)} %bitcast.37, f32[16,5,8,128]{3,2,1,0:T(8,128)S(1)} %bitcast.38, f32[96,5,8,128]{3,2,1,0:T(8,128)S(1)} %bitcast.33), custom_call_target="tpu_custom_call" | custom-call | tf_op jit(solution)/shard_map/relax/pallas_call | solution.py:509
  72.3 0.0 copy-start.3
  72.3 1.1 copy-done.3
  73.4 10.9 %swap_1.1 = (f32[16,5,8,128]{3,2,1,0:T(8,128)}, f32[16,5,8,128]{3,2,1,0:T(8,128)}) custom-call(f32[64,5,8,128]{3,2,1,0:T(8,128)} %copy-done.3), custom_call_target="tpu_custom_call" | custom-call | tf_op jit(solution)/shard_map/swap_1/pallas_call | solution.py:500
  84.2 0.0 copy-start.4
  84.2 1.3 copy-done.4
  85.6 1.0 copy-done.12
  86.5 1.0 copy-done.13
  87.5 15.3 %relax.4.times_ref.cur_ref = f32[64,5,8,128]{3,2,1,0:T(8,128)S(1)} custom-call(f32[2]{0:T(128)S(1)} %pad_maximum_fusion.fence_ref, f32[16,5,8,128]{3,2,1,0:T(8,128)S(1)} %copy-done.12, f32[64,5,8,128]{3,2,1,0:T(8,128)S(1)} %copy-done.4, f32[16,5,8,128]{3,2,1,0:T(8,128)S(1)} %copy-done.13, f32[96,5,8,128]{3,2,1,0:T(8,128)S(1)} %bitcast.34), custom_call_target="tpu_custom_call" | custom-call | tf_op jit(solution)/shard_map/relax/pallas_call | solution.py:509
  102.8 0.0 copy-start.1
  102.8 1.1 copy-done.1
  103.9 8.8 %swap_2.1 = (f32[16,5,8,128]{3,2,1,0:T(8,128)}, f32[16,5,8,128]{3,2,1,0:T(8,128)}) custom-call(f32[64,5,8,128]{3,2,1,0:T(8,128)} %copy-done.1), custom_call_target="tpu_custom_call" | custom-call | tf_op jit(solution)/shard_map/swap_2/pallas_call | solution.py:500
  112.7 0.0 copy-start.2
  112.8 1.3 copy-done.2
  114.1 1.0 copy-done.10
  115.0 1.0 copy-done.11
  116.0 15.3 %relax.5 = f32[64,5,8,128]{3,2,1,0:T(8,128)S(1)} custom-call(f32[2]{0:T(128)S(1)} %pad_maximum_fusion.fence_ref, f32[16,5,8,128]{3,2,1,0:T(8,128)S(1)} %copy-done.10, f32[64,5,8,128]{3,2,1,0:T(8,128)S(1)} %copy-done.2, f32[16,5,8,128]{3,2,1,0:T(8,128)S(1)} %copy-done.11, f32[96,5,8,128]{3,2,1,0:T(8,128)S(1)} %bitcast.35), custom_call_target="tpu_custom_call" | custom-call | tf_op jit(solution)/shard_map/relax/pallas_call | solution.py:509
  131.3 0.0 copy-done.17
  131.4 0.1 add_select_fusion.3
  131.4 7.8 %finish.1 = (f32[4,16,1280]{2,1,0:T(8,128)S(1)}, f32[4,8,128]{2,1,0:T(8,128)S(1)}) custom-call(s32[512]{0:T(512)S(1)} %get-tuple-element.45.spots_ref, s32[512]{0:T(512)S(1)} %get-tuple-element.44.turns_ref, f32[2560,128]{1,0:T(8,128)S(1)} %bitcast.36), custom_call_target="tpu_custom_call" | custom-call | tf_op jit(solution)/shard_map/finish/pallas_call | solution.py:532
  139.3 0.7 copy-done.9
  140.1 0.2 convert_reduce_fusion
  140.3 0.3 fusion
  140.7 0.1 reshape.121
  140.8 0.1 copy.25
  140.9 0.7 reshape.122.send_ref
  141.6 9.7 %deliver.1 = (f32[16,4096]{1,0:T(8,128)}, f32[16,1,256]{2,1,0:T(1,128)}) custom-call(f32[4,16,1280]{2,1,0:T(8,128)} %copy-done.9, f32[16,1,256]{2,1,0:T(1,128)} %reshape.122.send_ref), custom_call_target="tpu_custom_call" | custom-call | tf_op jit(solution)/shard_map/deliver/pallas_call | solution.py:568
  151.3 0.8 reduce
  152.0 0.1 reshape_squeeze.3
  152.3 0.7 reshape.123
  152.9 1.7 %copy.27 = f32[16,4096]{1,0:T(8,128)} copy(f32[16,4096]{1,0:T(8,128)} %get-tuple-element.48) | data formatting | bytes 524288
  (20 shorter events, 0.2 us)
Async XLA Ops:
  0.6 37.1 %copy-start.16 = (s32[4]{0:T(128)S(1)}, s32[4]{0:T(128)}, u32[]{:S(2)}) copy-start(s32[4]{0:T(128)} %cells_ref.1) | copy-start | bytes 52
  37.8 1.3 copy-start.5
  39.1 1.0 copy-start.6
  40.1 1.0 copy-start.7
  41.0 1.0 copy-start.8
  42.0 0.9 copy-start.14
  42.9 0.9 copy-start.15
  55.4 1.5 copy-start
  72.3 1.1 copy-start.3
  84.2 1.3 copy-start.4
  85.6 1.0 copy-start.12
  86.5 1.0 copy-start.13
  102.8 1.1 copy-start.1
  112.7 1.3 copy-start.2
  114.1 1.0 copy-start.10
  115.0 1.0 copy-start.11
  116.0 15.3 %copy-start.17 = (s32[4,2,1,128]{3,2,1,0:T(1,128)S(1)}, s32[4,2,1,128]{3,2,1,0:T(1,128)}, u32[]{:S(2)}) copy-start(s32[4,2,1,128]{3,2,1,0:T(1,128)} %get-tuple-element.19) | copy-start | bytes 12292
  139.3 0.7 copy-start.9

commit v3 on v2

--- a/solution.py
+++ b/solution.py
@@ -21,6 +21,7 @@
 LANES = 128
 SUBS = 8
 GROUP = 8
+EDGE = 4
 VMEM = pl.BlockSpec(memory_space=pltpu.VMEM)
 SMEM = pl.BlockSpec(memory_space=pltpu.SMEM)
 ANY = pl.BlockSpec(memory_space=pl.ANY)
@@ -74,111 +75,46 @@
     pl.semaphore_wait(barrier, others + below + above)
 
 
-def trade(me, below, above, downs, ups, send_sems, recv_sems):
-
-    def lower(n):
-        return remote(*downs[n], send_sems.at[0, n], recv_sems.at[0, n], me - SLAB)
-
-    def upper(n):
-        return remote(*ups[n], send_sems.at[1, n], recv_sems.at[1, n], me + SLAB)
-
-    def landed(side, n, dst, device):
-        remote(dst, dst, send_sems.at[side, n], recv_sems.at[side, n], device).wait_recv()
-
-    @pl.when(below)
-    def _():
-        for n in range(len(downs)):
-            lower(n).start()
-
-    @pl.when(above)
-    def _():
-        for n in range(len(ups)):
-            upper(n).start()
-
-    @pl.when(below)
-    def _():
-        for n in range(len(downs)):
-            lower(n).wait_send()
-            landed(1, n, ups[n][1], me - SLAB)
-
-    @pl.when(above)
-    def _():
-        for n in range(len(ups)):
-            upper(n).wait_send()
-            landed(0, n, downs[n][1], me + SLAB)
-
-
-def regroup(count, start_ref, cost_ref, info_ref, t_ref, c_ref, g_ref, pt, pc, nt, nc,
-            local_sems, send_sems, recv_sems, far_send, far_recv):
+def selection(phases, back):
+    size = phases * LANES
+    packed = lax.broadcasted_iota(jnp.int32, (size, size), 0 if back else 1)
+    plain = lax.broadcasted_iota(jnp.int32, (size, size), 1 if back else 0)
+    return jnp.where(plain == packed % LANES * phases + packed // LANES, 1.0, 0.0)
+
+
+def gather(count, first_ref, cells_ref, start_ref, cost_ref, info_ref, times_ref, packed_ref, g_ref,
+           choose, t_ref, c_ref, pc, nc, local_sems, send_sems, recv_sems, far_send, far_recv):
     me = lax.axis_index("space")
     base = me // SLAB * SLAB
     p = me % SLAB
-    size = start_ref.shape[2] // SLAB
-    window = t_ref.shape[3]
+    _, sources, rows, window = t_ref.shape
+    width = start_ref.shape[2]
+    size = width // SLAB
     barrier = pltpu.get_barrier_semaphore()
     for o in range(1, SLAB):
         signal(barrier, base + (p + o) % SLAB)
     below, above = greet(barrier, me, count)
     meet(barrier, me, count, SLAB - 1)
-
-    def pieces(q):
+    kinds = (c_ref, g_ref, t_ref)
+
+    def piece(q, n):
         cols = pl.ds(pl.multiple_of(window_start(q, size), LANES), window)
-        return (
-            (start_ref.at[:, :, cols], t_ref.at[p]),
-            (cost_ref.at[:, cols], c_ref.at[p]),
-            (info_ref, g_ref.at[p]),
-        )
-
-    def outgoing(o):
+        return (cost_ref.at[:, cols], info_ref, start_ref.at[:, :, cols])[n], kinds[n].at[p]
+
+    def outgoing(o, n):
         q = (p + o) % SLAB
-        return [
-            remote(src, dst, send_sems.at[o - 1, n], recv_sems.at[p, n], base + q)
-            for n, (src, dst) in enumerate(pieces(q))
-        ]
-
-    local = [
-        pltpu.make_async_copy(src, dst, local_sems.at[n]) for n, (src, dst) in enumerate(pieces(p))
-    ]
-    for o in (2, 1, 3):
-        for c in outgoing(o):
-            c.start()
-    for c in local:
-        c.start()
-    for c in local:
-        c.wait()
-    for o in range(1, SLAB):
+        return remote(*piece(q, n), send_sems.at[o - 1, n], recv_sems.at[p, n], base + q)
+
+    def arrived(o, n):
         q = (p + o) % SLAB
-        for n, ref in enumerate((t_ref, c_ref, g_ref)):
-            remote(ref.at[q], ref.at[q], send_sems.at[o - 1, n], recv_sems.at[q, n], base + q).wait_recv()
-    trade(me, below, above,
-          ((t_ref.at[0], nt), (c_ref.at[0], nc)),
-          ((t_ref.at[SLAB - 1], pt), (c_ref.at[SLAB - 1], pc)), far_send, far_recv)
-    for o in range(1, SLAB):
-        for c in outgoing(o):
-            c.wait_send()
-
-
-def swap(count, times_ref, prev_ref, next_ref, far_send, far_recv):
-    me = lax.axis_index("space")
-    barrier = pltpu.get_barrier_semaphore()
-    below, above = greet(barrier, me, count)
-    meet(barrier, me, count, 0)
-    rows = times_ref.shape[0]
-    trade(me, below, above,
-          ((times_ref.at[pl.ds(0, HALO)], next_ref),),
-          ((times_ref.at[pl.ds(rows - HALO, HALO)], prev_ref),), far_send, far_recv)
-
-
-def selection(phases, back):
-    size = phases * LANES
-    packed = lax.broadcasted_iota(jnp.int32, (size, size), 0 if back else 1)
-    plain = lax.broadcasted_iota(jnp.int32, (size, size), 1 if back else 0)
-    return jnp.where(plain == packed % LANES * phases + packed // LANES, 1.0, 0.0)
-
-
-def prepare(width, first_ref, cells_ref, fence_ref, t_ref, c_ref, pt, pc, nt, nc, times_ref,
-            packed_ref, choose):
-    _, sources, rows, window = t_ref.shape
+        ref = kinds[n].at[q]
+        remote(ref, ref, send_sems.at[o - 1, n], recv_sems.at[q, n], base + q).wait_recv()
+
+    local = [pltpu.make_async_copy(*piece(p, n), local_sems.at[n]) for n in range(3)]
+    for n in range(3):
+        for o in (2, 1, 3):
+            outgoing(o, n).start()
+        local[n].start()
     half = window // 2
     phases = half // LANES
     choose[...] = selection(phases, False)
@@ -186,47 +122,78 @@
     col = lax.broadcasted_iota(jnp.int32, (rows, half), 1)
     place = row * width + col
     far = jnp.float32(far_value)
+    chunk = rows * phases * SUBS
 
     def arrange(x):
         return jnp.dot(
             x, choose[...], precision=lax.Precision.HIGHEST, preferred_element_type=jnp.float32
         )
 
-    def put(ref, block, h, s, y, k):
-        start = (block * rows * phases + k) * SUBS + s * 2 + h
-        ref[pl.ds(start, rows, stride=phases * SUBS), :] = y
-
-    for block in range(SLAB + 2):
-        outside = None
-        if block in (0, SLAB + 1):
-            outside = fence_ref[0 if block == 0 else 1] > 0.0
+    def put(ref, start, n, y):
+        for k in range(phases):
+            ref[pl.ds(start + k * SUBS + n, rows, stride=phases * SUBS), :] = y[:, k * LANES : (k + 1) * LANES]
+
+    def pack_times(q):
         for h in range(2):
             cols = slice(h * half, (h + 1) * half)
             xs = []
             for s in range(sources):
-                if block == 0:
-                    x = pt[s, :, cols]
-                elif block == SLAB + 1:
-                    x = nt[s, :, cols]
-                else:
-                    x = t_ref[block - 1, s, :, cols]
-                offset = cells_ref[s] - (first_ref[0] + (block - 1) * rows * width + h * half)
-                x = jnp.where(place == offset, 0.0, x)
-                xs.append(x)
-            if block == 0:
-                c = pc[:, cols]
-            elif block == SLAB + 1:
-                c = nc[:, cols]
-            else:
-                c = c_ref[block - 1, :, cols]
-            xs.append(c)
-            if outside is not None:
-                xs = [jnp.where(outside, far, x) for x in xs]
+                offset = cells_ref[s] - (first_ref[0] + q * (rows * width) + h * half)
+                xs.append(jnp.where(place == offset, 0.0, t_ref[q, s, :, cols]))
             y = arrange(jnp.concatenate(xs, axis=0))
-            for k in range(phases):
+            for s in range(sources):
+                put(times_ref, q * chunk, s * 2 + h, y[s * rows : (s + 1) * rows])
+
+    def pack_costs(xs, starts):
+        for h in range(2):
+            y = arrange(jnp.concatenate([x[:, h * half : (h + 1) * half] for x in xs], axis=0))
+            for n, start in enumerate(starts):
                 for s in range(sources):
-                    put(times_ref, block, h, s, y[s * rows : (s + 1) * rows, k * LANES : (k + 1) * LANES], k)
-                    put(packed_ref, block, h, s, y[sources * rows :, k * LANES : (k + 1) * LANES], k)
+                    put(packed_ref, start, s * 2 + h, y[n * rows : (n + 1) * rows])
+
+    local[2].wait()
+    pack_times(p)
+    local[0].wait()
+    local[1].wait()
+    for o in range(1, SLAB):
+        arrived(o, 0)
+        arrived(o, 1)
+
+    def lower():
+        return remote(c_ref.at[0], nc, far_send.at[0], far_recv.at[0], me - SLAB)
+
+    def upper():
+        return remote(c_ref.at[SLAB - 1], pc, far_send.at[1], far_recv.at[1], me + SLAB)
+
+    @pl.when(below)
+    def _():
+        lower().start()
+
+    @pl.when(above)
+    def _():
+        upper().start()
+
+    pack_costs([c_ref[q] for q in range(SLAB)], [(q + 1) * chunk for q in range(SLAB)])
+
+    @pl.when(below)
+    def _():
+        lower().wait_send()
+        remote(pc, pc, far_send.at[1], far_recv.at[1], me - SLAB).wait_recv()
+
+    @pl.when(above)
+    def _():
+        upper().wait_send()
+        remote(nc, nc, far_send.at[0], far_recv.at[0], me + SLAB).wait_recv()
+
+    pack_costs(
+        [jnp.where(below, pc[...], far), jnp.where(above, nc[...], far)], [0, (SLAB + 1) * chunk]
+    )
+    for o in (1, 3, 2):
+        arrived(o, 2)
+        pack_times((p + o) % SLAB)
+    for o in range(1, SLAB):
+        for n in range(3):
+            outgoing(o, n).wait_send()
 
 
 def edge_fixers():
@@ -247,52 +214,38 @@
     return from_left, from_right
 
 
-def relax_block(fence_ref, prev_ref, cur_ref, next_ref, cost_ref, out_ref, one, two, cost2, cost5):
-    rows, phases = cur_ref.shape[0], cur_ref.shape[1]
+def march(count, times_ref, cost_ref, out_ref, one, two, staged, landed, send_sems, recv_sems):
+    me = lax.axis_index("space")
+    barrier = pltpu.get_barrier_semaphore()
+    below, above = greet(barrier, me, count)
+    rows, phases = times_ref.shape[0], times_ref.shape[1]
     high = cost_ref.shape[0]
     total = phases + 4
     far = jnp.float32(far_value)
     from_left, from_right = edge_fixers()
 
-    def store_row(buf, r, vals):
-        for k in range(phases):
-            buf[r, 2 + k] = vals[k]
-        buf[r, 0] = from_left(vals[phases - 2])
-        buf[r, 1] = from_left(vals[phases - 1])
-        buf[r, phases + 2] = from_right(vals[0])
-        buf[r, phases + 3] = from_right(vals[1])
-
     @pl.loop(0, rows // 4)
     def _(g):
         for i in range(4):
-            r = 4 * g + i
-            store_row(one, HALO + r, [cur_ref[r, k] for k in range(phases)])
-
-    for ref, start, n in ((prev_ref, 0, 0), (next_ref, HALO + rows, 1)):
-
-        @pl.loop(0, HALO // 4)
-        def _(g):
-            for i in range(4):
-                r = 4 * g + i
-                vals = [jnp.where(fence_ref[n] > 0.0, far, ref[r, k]) for k in range(phases)]
-                store_row(one, start + r, vals)
-
-    @pl.loop(0, high // 4)
-    def _(g):
-        for i in range(4):
+            r = HALO + 4 * g + i
+            vals = [times_ref[4 * g + i, k] for k in range(phases)]
             for k in range(phases):
-                c = cost_ref[4 * g + i, k]
-                cost2[4 * g + i, k] = c * root_two
-                cost5[4 * g + i, k] = c * root_five
-
-    def sweep(src, dst, lowest):
-        groups = (high - 2 * lowest + GROUP - 1) // GROUP
+                one[r, 2 + k] = vals[k]
+            one[r, 0] = from_left(vals[phases - 2])
+            one[r, 1] = from_left(vals[phases - 1])
+            one[r, phases + 2] = from_right(vals[0])
+            one[r, phases + 3] = from_right(vals[1])
+
+    meet(barrier, me, count, 0)
+
+    def sweep(src, dst, lo, hi, size):
+        groups = (hi - lo + size - 1) // size
 
         def begin(group):
-            return jnp.minimum(lowest + GROUP * group, high - lowest - GROUP)
+            return jnp.minimum(lo + size * group, hi - size)
 
         def edges(start):
-            for i in range(GROUP):
+            for i in range(size):
                 r = start + i
                 dst[r, 0] = from_left(dst[r, phases])
                 dst[r, 1] = from_left(dst[r, phases + 1])
@@ -306,33 +259,95 @@
             t = {}
 
             def load(d):
-                inner = range(1, total - 1) if d in (-2, GROUP + 1) else range(total)
+                inner = range(1, total - 1) if d in (-2, size + 1) else range(total)
                 t[d] = {x: src[r0 + d, x] for x in inner}
 
             for d in (-2, -1, 0, 1):
                 load(d)
-            for i in range(GROUP):
+            for i in range(size):
                 load(i + 2)
                 r = r0 + i
                 m = t[i]
                 a = [jnp.minimum(t[i - 1][x], t[i + 1][x]) for x in range(total)]
                 b = {x: jnp.minimum(t[i - 2][x], t[i + 2][x]) for x in range(1, total - 1)}
                 for k in range(2, phases + 2):
+                    c = cost_ref[r, k - 2]
                     near = jnp.minimum(a[k], jnp.minimum(m[k - 1], m[k + 1]))
                     diag = jnp.minimum(a[k - 1], a[k + 1])
                     knight = jnp.minimum(
                         jnp.minimum(a[k - 2], a[k + 2]), jnp.minimum(b[k - 1], b[k + 1])
                     )
-                    best = jnp.minimum(near + cost_ref[r, k - 2], diag + cost2[r, k - 2])
-                    best = jnp.minimum(best, knight + cost5[r, k - 2])
+                    best = jnp.minimum(near + c, diag + c * root_two)
+                    best = jnp.minimum(best, knight + c * root_five)
                     dst[r, k] = jnp.minimum(m[k], best)
 
         edges(begin(groups - 1))
 
-    @pl.loop(0, SWEEPS // 2)
-    def _(step):
-        sweep(one, two, 4 * step + 2)
-        sweep(two, one, 4 * step + 4)
+    def inner(src, dst, j):
+        sweep(src, dst, HALO + 4 * j, high - HALO - 4 * j, GROUP)
+
+    def outer(src, dst, j):
+        sweep(src, dst, 2 * j, HALO + 4 * j, EDGE)
+        sweep(src, dst, high - HALO - 4 * j, high - 2 * j, EDGE)
+
+    last = (rows - GROUP) // 8
+
+    @pl.loop(0, BLOCKS)
+    def _(block):
+        def down():
+            return remote(staged.at[0], landed.at[block, 1], send_sems.at[block, 0],
+                          recv_sems.at[block, 1], me - SLAB)
+
+        def up():
+            return remote(staged.at[1], landed.at[block, 0], send_sems.at[block, 1],
+                          recv_sems.at[block, 0], me + SLAB)
+
+        @pl.loop(0, HALO)
+        def _(r):
+            for x in range(total):
+                staged[0, r, x] = one[HALO + r, x]
+                staged[1, r, x] = one[high - 2 * HALO + r, x]
+
+        @pl.when(below)
+        def _():
+            down().start()
+
+        @pl.when(above)
+        def _():
+            up().start()
+
+        inner_pairs = min(SWEEPS, last) // 2
+
+        @pl.loop(0, inner_pairs)
+        def _(step):
+            inner(one, two, 2 * step + 1)
+            inner(two, one, 2 * step + 2)
+
+        for j in range(2 * inner_pairs + 1, min(SWEEPS, last) + 1):
+            inner(one, two, j)
+
+        @pl.when(below)
+        def _():
+            down().wait_send()
+            remote(landed.at[block, 0], landed.at[block, 0], send_sems.at[block, 0],
+                   recv_sems.at[block, 0], me - SLAB).wait_recv()
+
+        @pl.when(above)
+        def _():
+            up().wait_send()
+            remote(landed.at[block, 1], landed.at[block, 1], send_sems.at[block, 1],
+                   recv_sems.at[block, 1], me + SLAB).wait_recv()
+
+        @pl.loop(0, HALO)
+        def _(r):
+            for x in range(total):
+                one[r, x] = jnp.where(below, landed[block, 0, r, x], far)
+                one[high - HALO + r, x] = jnp.where(above, landed[block, 1, r, x], far)
+
+        @pl.loop(0, SWEEPS // 2)
+        def _(step):
+            outer(one, two, 2 * step + 1)
+            outer(two, one, 2 * step + 2)
 
     @pl.loop(0, rows)
     def _(r):
@@ -458,68 +473,51 @@
 
     cost = jnp.where(ocean == 1, slowness, jnp.float32(land_cost))
     info = jnp.stack([gauge_cells, gauge_owner[:, 0]])[:, None, :]
-    fence = jnp.stack([jnp.where(slab == 0, 1.0, 0.0), jnp.where(slab == count // SLAB - 1, 1.0, 0.0)])
-    fence = fence.astype(f32)
     first = (slab * (SLAB * rows * width) + left).astype(jnp.int32).reshape(1)
     dma = pltpu.SemaphoreType.DMA
 
-    piece_t = jax.ShapeDtypeStruct((sources, rows, window), f32)
-    piece_c = jax.ShapeDtypeStruct((rows, window), f32)
-    t4, c4, g4, pt, pc, nt, nc = pl.pallas_call(
-        functools.partial(regroup, count),
+    times, packed, g4 = pl.pallas_call(
+        functools.partial(gather, count),
         out_shape=(
-            jax.ShapeDtypeStruct((SLAB,) + piece_t.shape, f32),
-            jax.ShapeDtypeStruct((SLAB,) + piece_c.shape, f32),
+            jax.ShapeDtypeStruct((SLAB * rows * phases * SUBS, LANES), f32),
+            jax.ShapeDtypeStruct((high * phases * SUBS, LANES), f32),
             jax.ShapeDtypeStruct((SLAB,) + info.shape, jnp.int32),
-            piece_t, piece_c, piece_t, piece_c,
         ),
-        in_specs=[ANY] * 3,
-        out_specs=(ANY,) * 7,
-        scratch_shapes=[dma((3,)), dma((SLAB - 1, 3)), dma((SLAB, 3)), dma((2, 2)), dma((2, 2))],
-        compiler_params=pltpu.CompilerParams(collective_id=0, has_side_effects=True),
-        name="regroup",
-    )(start_times, cost, info)
-
-    flat = jax.ShapeDtypeStruct((high * phases * SUBS, LANES), f32)
-    times, packed = pl.pallas_call(
-        functools.partial(prepare, width),
-        out_shape=(flat, flat),
-        in_specs=[SMEM] * 3 + [VMEM] * 6,
-        out_specs=(VMEM, VMEM),
-        scratch_shapes=[pltpu.VMEM((half, half), f32)],
-        compiler_params=PARAMS,
-        name="prepare",
-    )(first, source_cells, fence, t4, c4, pt, pc, nt, nc)
-    packed = packed.reshape(high, phases, SUBS, LANES)
-    times = times.reshape(high, phases, SUBS, LANES)
-    prev, times, following = times[:HALO], times[HALO : high - HALO], times[high - HALO :]
-
-    for block in range(BLOCKS):
-        if block:
-            halo = jax.ShapeDtypeStruct((HALO,) + times.shape[1:], f32)
-            prev, following = pl.pallas_call(
-                functools.partial(swap, count),
-                out_shape=(halo, halo),
-                in_specs=[ANY],
-                out_specs=(ANY, ANY),
-                scratch_shapes=[dma((2, 1)), dma((2, 1))],
-                compiler_params=pltpu.CompilerParams(collective_id=block, has_side_effects=True),
-                name=f"swap_{block}",
-            )(times)
-        times = pl.pallas_call(
-            relax_block,
-            out_shape=jax.ShapeDtypeStruct(times.shape, f32),
-            in_specs=[SMEM, VMEM, VMEM, VMEM, VMEM],
-            out_specs=VMEM,
-            scratch_shapes=[
-                pltpu.VMEM((high, phases + 4, SUBS, LANES), f32),
-                pltpu.VMEM((high, phases + 4, SUBS, LANES), f32),
-                pltpu.VMEM((high, phases, SUBS, LANES), f32),
-                pltpu.VMEM((high, phases, SUBS, LANES), f32),
-            ],
-            compiler_params=PARAMS,
-            name="relax",
-        )(fence, prev, times, following, packed)
+        in_specs=[SMEM, SMEM, ANY, ANY, ANY],
+        out_specs=(VMEM, VMEM, ANY),
+        scratch_shapes=[
+            pltpu.VMEM((half, half), f32),
+            pltpu.VMEM((SLAB, sources, rows, window), f32),
+            pltpu.VMEM((SLAB, rows, window), f32),
+            pltpu.VMEM((rows, window), f32),
+            pltpu.VMEM((rows, window), f32),
+            dma((3,)), dma((SLAB - 1, 3)), dma((SLAB, 3)), dma((2,)), dma((2,)),
+        ],
+        compiler_params=pltpu.CompilerParams(
+            collective_id=0, has_side_effects=True, vmem_limit_bytes=48 * 1024 * 1024
+        ),
+        name="gather",
+    )(first, source_cells, start_times, cost, info)
+
+    grid = (SLAB * rows, phases, SUBS, LANES)
+    edged = (phases + 4, SUBS, LANES)
+    times = pl.pallas_call(
+        functools.partial(march, count),
+        out_shape=jax.ShapeDtypeStruct(grid, f32),
+        in_specs=[VMEM, VMEM],
+        out_specs=VMEM,
+        scratch_shapes=[
+            pltpu.VMEM((high,) + edged, f32),
+            pltpu.VMEM((high,) + edged, f32),
+            pltpu.VMEM((2, HALO) + edged, f32),
+            pltpu.VMEM((BLOCKS, 2, HALO) + edged, f32),
+            dma((BLOCKS, 2)), dma((BLOCKS, 2)),
+        ],
+        compiler_params=pltpu.CompilerParams(
+            collective_id=1, has_side_effects=True, vmem_limit_bytes=48 * 1024 * 1024
+        ),
+        name="march",
+    )(times.reshape(grid), packed.reshape((high,) + grid[1:]))
 
     cells, owners = g4[:, 0, 0], g4[:, 1, 0]
     column = cells % width

time: 155 us -> 138 us (0.89)
  local copies, waits for them, and re-layouts: 20.4 us -> 6.03 us
    unnamed x37 -> x7, local copies, waits for them, and re-layouts: 18.5 us -> 4.26 us
    pallas_call x7 -> x2, Pallas kernels: 111 us -> 111 us  [the longest x1 84.6 us: on_device(): pl.pallas_call(functools.partial(march, count), out_shape=jax.ShapeDtypeS...]
where the time goes in v3:
time: 138 us
  Pallas kernels  128 us (93%)
  local copies, waits for them, and re-layouts  6.03 us (4%)
  other arithmetic  2.91 us (2%)
    pallas_call x1, Pallas kernels, on_device(): pl.pallas_call(functools.partial(march, count), out_shape=jax.ShapeDtypeS...  84.6 us
    pallas_call x1, Pallas kernels, on_device(): pl.pallas_call(functools.partial(gather, count), out_shape=(jax.ShapeDtyp...  26.1 us
    pallas_call x1, Pallas kernels, on_device(): pl.pallas_call(functools.partial(deliver, count, size), out_shape=(jax.Sh...  9.11 us
    pallas_call x1, Pallas kernels, on_device(): pl.pallas_call(finish, out_shape=(jax.ShapeDtypeStruct((SLAB, rows, windo...  7.84 us
    unnamed x7, local copies, waits for them, and re-layouts  4.26 us

profile of v3, /device:TPU:0, one launch (start us, length us, event | category | flops | bytes accessed | tf_op | source)
XLA Modules:
  0.0 137.6 jit_solution(5293837984608246709)
XLA Ops:
  0.7 1.1 compare_select_fusion.cost_ref
  1.8 0.7 pad_add_fusion
  2.4 0.0 copy-start
  2.4 1.2 copy-done
  3.7 0.0 copy-start.2
  3.7 0.7 copy-done.2
  4.3 26.1 %gather.1 = (f32[2560,128]{1,0:T(8,128)S(1)}, f32[3840,128]{1,0:T(8,128)S(1)}, s32[4,2,1,128]{3,2,1,0:T(1,128)S(1)}) custom-call(s32[1]{0:T(128)} %bitcast.1.first_ref, s32[4]{0:T(128)S(1)} %copy-done.2, f32[4,16,4096]{2,1,0:T(8,128)S(1)} %copy-done, f32[16,4096]{1,0:T(8,128)S(1)} %compare_select_fusion.cost_ref, s32[2,1,128]{2,1,0:T(1,128)S(1)} %bitcast.33), custom_call_target="tpu_custom_call" | custom-call | tf_op jit(solution)/shard_map/gather/pallas_call | solution.py:479
  30.4 0.2 convert_reduce_fusion
  30.7 84.6 %march.1 = f32[64,5,8,128]{3,2,1,0:T(8,128)S(1)} custom-call(f32[64,5,8,128]{3,2,1,0:T(8,128)S(1)} %bitcast.31, f32[96,5,8,128]{3,2,1,0:T(8,128)S(1)} %bitcast.30), custom_call_target="tpu_custom_call" | custom-call | tf_op jit(solution)/shard_map/march/pallas_call | solution.py:504
  115.3 0.1 add_select_fusion.3
  115.3 7.8 %finish.1 = (f32[4,16,1280]{2,1,0:T(8,128)S(1)}, f32[4,8,128]{2,1,0:T(8,128)S(1)}) custom-call(s32[512]{0:T(512)S(1)} %get-tuple-element.23.spots_ref, s32[512]{0:T(512)S(1)} %get-tuple-element.22.turns_ref, f32[2560,128]{1,0:T(8,128)S(1)} %bitcast.29), custom_call_target="tpu_custom_call" | custom-call | tf_op jit(solution)/shard_map/finish/pallas_call | solution.py:530
  123.2 0.0 copy-start.1
  123.2 0.7 copy-done.1
  123.9 0.3 fusion
  124.3 0.1 reshape.121
  124.4 0.1 copy.25
  124.5 0.7 reshape.122.send_ref
  125.2 9.1 %deliver.1 = (f32[16,4096]{1,0:T(8,128)}, f32[16,1,256]{2,1,0:T(1,128)}) custom-call(f32[4,16,1280]{2,1,0:T(8,128)} %copy-done.1, f32[16,1,256]{2,1,0:T(1,128)} %reshape.122.send_ref), custom_call_target="tpu_custom_call" | custom-call | tf_op jit(solution)/shard_map/deliver/pallas_call | solution.py:566
  134.3 0.8 reduce
  135.1 0.1 reshape_squeeze.3
  135.3 0.7 reshape.123
  136.0 1.7 %copy.27 = f32[16,4096]{1,0:T(8,128)} copy(f32[16,4096]{1,0:T(8,128)} %get-tuple-element.26) | data formatting | bytes 524288
  (8 shorter events, 0.1 us)
Async XLA Ops:
  2.4 1.2 copy-start
  3.7 0.7 copy-start.2
  123.2 0.7 copy-start.1

commit v4 on v3

--- a/solution.py
+++ b/solution.py
@@ -22,6 +22,7 @@
 SUBS = 8
 GROUP = 8
 EDGE = 4
+UNROLL = 32
 VMEM = pl.BlockSpec(memory_space=pltpu.VMEM)
 SMEM = pl.BlockSpec(memory_space=pltpu.SMEM)
 ANY = pl.BlockSpec(memory_space=pl.ANY)
@@ -214,7 +215,8 @@
     return from_left, from_right
 
 
-def march(count, times_ref, cost_ref, out_ref, one, two, staged, landed, send_sems, recv_sems):
+def march(count, times_ref, cost_ref, out_ref, one, two, one_edge, two_edge, staged, landed,
+          send_sems, recv_sems):
     me = lax.axis_index("space")
     barrier = pltpu.get_barrier_semaphore()
     below, above = greet(barrier, me, count)
@@ -223,72 +225,85 @@
     total = phases + 4
     far = jnp.float32(far_value)
     from_left, from_right = edge_fixers()
-
-    @pl.loop(0, rows // 4)
+    first, second = (one, one_edge), (two, two_edge)
+
+    def edges(field, start, size):
+        body, edge = field
+        for i in range(size):
+            r = start + i
+            edge[r, 0] = from_left(body[r, phases - 2])
+            edge[r, 1] = from_left(body[r, phases - 1])
+            edge[r, 2] = from_right(body[r, 0])
+            edge[r, 3] = from_right(body[r, 1])
+
+    def enter(r, vals):
+        for k in range(phases):
+            one[r, k] = vals[k]
+        one_edge[r, 0] = from_left(vals[phases - 2])
+        one_edge[r, 1] = from_left(vals[phases - 1])
+        one_edge[r, 2] = from_right(vals[0])
+        one_edge[r, 3] = from_right(vals[1])
+
+    @pl.loop(0, rows // 8)
     def _(g):
-        for i in range(4):
-            r = HALO + 4 * g + i
-            vals = [times_ref[4 * g + i, k] for k in range(phases)]
-            for k in range(phases):
-                one[r, 2 + k] = vals[k]
-            one[r, 0] = from_left(vals[phases - 2])
-            one[r, 1] = from_left(vals[phases - 1])
-            one[r, phases + 2] = from_right(vals[0])
-            one[r, phases + 3] = from_right(vals[1])
+        for i in range(8):
+            enter(HALO + 8 * g + i, [times_ref[8 * g + i, k] for k in range(phases)])
 
     meet(barrier, me, count, 0)
 
-    def sweep(src, dst, lo, hi, size):
-        groups = (hi - lo + size - 1) // size
-
-        def begin(group):
-            return jnp.minimum(lo + size * group, hi - size)
-
-        def edges(start):
-            for i in range(size):
-                r = start + i
-                dst[r, 0] = from_left(dst[r, phases])
-                dst[r, 1] = from_left(dst[r, phases + 1])
-                dst[r, phases + 2] = from_right(dst[r, 2])
-                dst[r, phases + 3] = from_right(dst[r, 3])
+    def relax(src, dst, r0, size):
+        body, edge = src
+        t = {}
+
+        def value(r, x):
+            if x < 2:
+                return edge[r, x]
+            return edge[r, x - phases] if x >= phases + 2 else body[r, x - 2]
+
+        def load(d):
+            inner = range(1, total - 1) if d in (-2, size + 1) else range(total)
+            t[d] = {x: value(r0 + d, x) for x in inner}
+
+        for d in (-2, -1, 0, 1):
+            load(d)
+        for i in range(size):
+            load(i + 2)
+            r = r0 + i
+            m = t[i]
+            a = [jnp.minimum(t[i - 1][x], t[i + 1][x]) for x in range(total)]
+            b = {x: jnp.minimum(t[i - 2][x], t[i + 2][x]) for x in range(1, total - 1)}
+            for k in range(2, phases + 2):
+                c = cost_ref[r, k - 2]
+                near = jnp.minimum(a[k], jnp.minimum(m[k - 1], m[k + 1]))
+                diag = jnp.minimum(a[k - 1], a[k + 1])
+                knight = jnp.minimum(
+                    jnp.minimum(a[k - 2], a[k + 2]), jnp.minimum(b[k - 1], b[k + 1])
+                )
+                best = jnp.minimum(near + c, diag + c * root_two)
+                best = jnp.minimum(best, knight + c * root_five)
+                dst[0][r, k - 2] = jnp.minimum(m[k], best)
+
+    def sweep(src, dst, starts, length, size):
+        groups = (length + size - 1) // size
+
+        def offset(group):
+            return jnp.minimum(size * group, length - size)
 
         @pl.loop(0, groups)
         def _(group):
-            r0 = begin(group)
-            edges(begin(jnp.maximum(group - 1, 0)))
-            t = {}
-
-            def load(d):
-                inner = range(1, total - 1) if d in (-2, size + 1) else range(total)
-                t[d] = {x: src[r0 + d, x] for x in inner}
-
-            for d in (-2, -1, 0, 1):
-                load(d)
-            for i in range(size):
-                load(i + 2)
-                r = r0 + i
-                m = t[i]
-                a = [jnp.minimum(t[i - 1][x], t[i + 1][x]) for x in range(total)]
-                b = {x: jnp.minimum(t[i - 2][x], t[i + 2][x]) for x in range(1, total - 1)}
-                for k in range(2, phases + 2):
-                    c = cost_ref[r, k - 2]
-                    near = jnp.minimum(a[k], jnp.minimum(m[k - 1], m[k + 1]))
-                    diag = jnp.minimum(a[k - 1], a[k + 1])
-                    knight = jnp.minimum(
-                        jnp.minimum(a[k - 2], a[k + 2]), jnp.minimum(b[k - 1], b[k + 1])
-                    )
-                    best = jnp.minimum(near + c, diag + c * root_two)
-                    best = jnp.minimum(best, knight + c * root_five)
-                    dst[r, k] = jnp.minimum(m[k], best)
-
-        edges(begin(groups - 1))
+            for start in starts:
+                edges(dst, start + offset(jnp.maximum(group - 1, 0)), size)
+            for start in starts:
+                relax(src, dst, start + offset(group), size)
+
+        for start in starts:
+            edges(dst, start + offset(groups - 1), size)
 
     def inner(src, dst, j):
-        sweep(src, dst, HALO + 4 * j, high - HALO - 4 * j, GROUP)
+        sweep(src, dst, [HALO + 4 * j], rows - 8 * j, GROUP)
 
     def outer(src, dst, j):
-        sweep(src, dst, 2 * j, HALO + 4 * j, EDGE)
-        sweep(src, dst, high - HALO - 4 * j, high - 2 * j, EDGE)
+        sweep(src, dst, [2 * j, high - HALO - 4 * j], HALO + 2 * j, EDGE)
 
     last = (rows - GROUP) // 8
 
@@ -302,11 +317,13 @@
             return remote(staged.at[1], landed.at[block, 0], send_sems.at[block, 1],
                           recv_sems.at[block, 0], me + SLAB)
 
-        @pl.loop(0, HALO)
-        def _(r):
-            for x in range(total):
-                staged[0, r, x] = one[HALO + r, x]
-                staged[1, r, x] = one[high - 2 * HALO + r, x]
+        @pl.loop(0, HALO // 4)
+        def _(g):
+            for i in range(4):
+                r = 4 * g + i
+                for k in range(phases):
+                    staged[0, r, k] = one[HALO + r, k]
+                    staged[1, r, k] = one[high - 2 * HALO + r, k]
 
         @pl.when(below)
         def _():
@@ -320,11 +337,11 @@
 
         @pl.loop(0, inner_pairs)
         def _(step):
-            inner(one, two, 2 * step + 1)
-            inner(two, one, 2 * step + 2)
+            inner(first, second, 2 * step + 1)
+            inner(second, first, 2 * step + 2)
 
         for j in range(2 * inner_pairs + 1, min(SWEEPS, last) + 1):
-            inner(one, two, j)
+            inner(first, second, j)
 
         @pl.when(below)
         def _():
@@ -338,21 +355,26 @@
             remote(landed.at[block, 1], landed.at[block, 1], send_sems.at[block, 1],
                    recv_sems.at[block, 1], me + SLAB).wait_recv()
 
-        @pl.loop(0, HALO)
-        def _(r):
-            for x in range(total):
-                one[r, x] = jnp.where(below, landed[block, 0, r, x], far)
-                one[high - HALO + r, x] = jnp.where(above, landed[block, 1, r, x], far)
+        @pl.loop(0, HALO // 4)
+        def _(g):
+            for i in range(4):
+                r = 4 * g + i
+                enter(r, [jnp.where(below, landed[block, 0, r, k], far) for k in range(phases)])
+                enter(
+                    high - HALO + r,
+                    [jnp.where(above, landed[block, 1, r, k], far) for k in range(phases)],
+                )
 
         @pl.loop(0, SWEEPS // 2)
         def _(step):
-            outer(one, two, 2 * step + 1)
-            outer(two, one, 2 * step + 2)
-
-    @pl.loop(0, rows)
-    def _(r):
-        for k in range(phases):
-            out_ref[r, k] = one[HALO + r, 2 + k]
+            outer(first, second, 2 * step + 1)
+            outer(second, first, 2 * step + 2)
+
+    @pl.loop(0, rows // 8)
+    def _(g):
+        for i in range(8):
+            for k in range(phases):
+                out_ref[8 * g + i, k] = one[HALO + 8 * g + i, k]
 
 
 def finish(spots_ref, turns_ref, times_ref, arrival_ref, gauge_ref, least, choose):
@@ -363,10 +385,10 @@
     steps = slab * rows * phases
     lane = lax.broadcasted_iota(jnp.int32, (SUBS, LANES), 1)
 
-    @pl.loop(0, steps // SUBS)
+    @pl.loop(0, steps // UNROLL)
     def _(group):
-        for i in range(SUBS):
-            row = pl.ds(pl.multiple_of((group * SUBS + i) * SUBS, SUBS), SUBS)
+        for i in range(UNROLL):
+            row = pl.ds(pl.multiple_of((group * UNROLL + i) * SUBS, SUBS), SUBS)
             x = times_ref[row, :]
             x = jnp.minimum(x, pltpu.roll(x, 2, 0))
             least[row, :] = jnp.minimum(x, pltpu.roll(x, 4, 0))
@@ -386,15 +408,15 @@
         for start in range(0, gauges, LANES):
 
             def step(group, acc):
-                for i in range(SUBS):
-                    n = group * SUBS + i
+                for i in range(UNROLL):
+                    n = group * UNROLL + i
                     g = b * gauges + start + n
                     x = times_ref[pl.ds(pl.multiple_of(spots_ref[g], SUBS), SUBS), :]
                     x = pltpu.roll(x, turns_ref[g], 1)
                     acc = jnp.where(lane == n, x, acc)
                 return acc
 
-            acc = lax.fori_loop(0, LANES // SUBS, step, jnp.zeros((SUBS, LANES), jnp.float32))
+            acc = lax.fori_loop(0, LANES // UNROLL, step, jnp.zeros((SUBS, LANES), jnp.float32))
             gauge_ref[b, :, start : start + LANES] = acc
 
 
@@ -500,17 +522,19 @@
     )(first, source_cells, start_times, cost, info)
 
     grid = (SLAB * rows, phases, SUBS, LANES)
-    edged = (phases + 4, SUBS, LANES)
+    edge = (4, SUBS, LANES)
     times = pl.pallas_call(
         functools.partial(march, count),
         out_shape=jax.ShapeDtypeStruct(grid, f32),
         in_specs=[VMEM, VMEM],
         out_specs=VMEM,
         scratch_shapes=[
-            pltpu.VMEM((high,) + edged, f32),
-            pltpu.VMEM((high,) + edged, f32),
-            pltpu.VMEM((2, HALO) + edged, f32),
-            pltpu.VMEM((BLOCKS, 2, HALO) + edged, f32),
+            pltpu.VMEM((high,) + grid[1:], f32),
+            pltpu.VMEM((high,) + grid[1:], f32),
+            pltpu.VMEM((high,) + edge, f32),
+            pltpu.VMEM((high,) + edge, f32),
+            pltpu.VMEM((2, HALO) + grid[1:], f32),
+            pltpu.VMEM((BLOCKS, 2, HALO) + grid[1:], f32),
             dma((BLOCKS, 2)), dma((BLOCKS, 2)),
         ],
         compiler_params=pltpu.CompilerParams(

time: 138 us -> 106 us (0.77)
  Pallas kernels: 128 us -> 95.7 us
    pallas_call x1, Pallas kernels: 84.6 us -> 55.3 us  [on_device(): pl.pallas_call(functools.partial(march, count), out_shape=jax.ShapeDtypeS...]
    pallas_call x1, Pallas kernels: 7.84 us -> 4.41 us  [on_device(): pl.pallas_call(finish, out_shape=(jax.ShapeDtypeStruct((SLAB, rows, windo...]
where the time goes in v4:
time: 106 us
  Pallas kernels  95.7 us (90%)
  local copies, waits for them, and re-layouts  6.02 us (6%)
  other arithmetic  2.91 us (3%)
    pallas_call x1, Pallas kernels, on_device(): pl.pallas_call(functools.partial(march, count), out_shape=jax.ShapeDtypeS...  55.3 us
    pallas_call x1, Pallas kernels, on_device(): pl.pallas_call(functools.partial(gather, count), out_shape=(jax.ShapeDtyp...  26.1 us
    pallas_call x1, Pallas kernels, on_device(): pl.pallas_call(functools.partial(deliver, count, size), out_shape=(jax.Sh...  9.84 us
    pallas_call x1, Pallas kernels, on_device(): pl.pallas_call(finish, out_shape=(jax.ShapeDtypeStruct((SLAB, rows, windo...  4.41 us
    unnamed x7, local copies, waits for them, and re-layouts  4.26 us

profile of v4, /device:TPU:0, one launch (start us, length us, event | category | flops | bytes accessed | tf_op | source)
XLA Modules:
  0.0 105.7 jit_solution(5604946144825791795)
XLA Ops:
  0.7 1.1 %compare_select_fusion.cost_ref = f32[16,4096]{1,0:T(8,128)S(1)} fusion(f32[16,4096]{1,0:T(8,128)} %param.6, s32[16,4096]{1,0:T(8,128)} %param.7), kind=kLoop, calls=%fused_computation.4 | loop fusion | flops 131072 | bytes 786432 | tf_op jit(solution)/shard_map/jit(_where)/select_n | solution.py:496
  1.8 0.7 pad_add_fusion
  2.4 0.0 copy-start
  2.4 1.2 %copy-done = f32[4,16,4096]{2,1,0:T(8,128)S(1)} copy-done((f32[4,16,4096]{2,1,0:T(8,128)S(1)}, f32[4,16,4096]{2,1,0:T(8,128)}, u32[]{:S(2)}) %copy-start) | copy-done | bytes 1048600
  3.7 0.0 copy-start.2
  3.7 0.7 copy-done.2
  4.3 26.1 %gather.1 = (f32[2560,128]{1,0:T(8,128)S(1)}, f32[3840,128]{1,0:T(8,128)S(1)}, s32[4,2,1,128]{3,2,1,0:T(1,128)S(1)}) custom-call(s32[1]{0:T(128)} %bitcast.1.first_ref, s32[4]{0:T(128)S(1)} %copy-done.2, f32[4,16,4096]{2,1,0:T(8,128)S(1)} %copy-done, f32[16,4096]{1,0:T(8,128)S(1)} %compare_select_fusion.cost_ref, s32[2,1,128]{2,1,0:T(1,128)S(1)} %bitcast.33), custom_call_target="tpu_custom_call" | custom-call | tf_op jit(solution)/shard_map/gather/pallas_call | solution.py:501
  30.4 0.2 convert_reduce_fusion
  30.7 55.3 %march.1 = f32[64,5,8,128]{3,2,1,0:T(8,128)S(1)} custom-call(f32[64,5,8,128]{3,2,1,0:T(8,128)S(1)} %bitcast.31, f32[96,5,8,128]{3,2,1,0:T(8,128)S(1)} %bitcast.30), custom_call_target="tpu_custom_call" | custom-call | tf_op jit(solution)/shard_map/march/pallas_call | solution.py:526
  86.0 0.1 add_select_fusion.3
  86.1 4.4 %finish.1 = (f32[4,16,1280]{2,1,0:T(8,128)S(1)}, f32[4,8,128]{2,1,0:T(8,128)S(1)}) custom-call(s32[512]{0:T(512)S(1)} %get-tuple-element.23.spots_ref, s32[512]{0:T(512)S(1)} %get-tuple-element.22.turns_ref, f32[2560,128]{1,0:T(8,128)S(1)} %bitcast.29), custom_call_target="tpu_custom_call" | custom-call | tf_op jit(solution)/shard_map/finish/pallas_call | solution.py:554
  90.5 0.0 copy-start.1
  90.5 0.7 copy-done.1
  91.3 0.3 fusion
  91.6 0.1 reshape.121
  91.8 0.1 copy.25
  91.8 0.7 reshape.122.send_ref
  92.6 9.8 %deliver.1 = (f32[16,4096]{1,0:T(8,128)}, f32[16,1,256]{2,1,0:T(1,128)}) custom-call(f32[4,16,1280]{2,1,0:T(8,128)} %copy-done.1, f32[16,1,256]{2,1,0:T(1,128)} %reshape.122.send_ref), custom_call_target="tpu_custom_call" | custom-call | tf_op jit(solution)/shard_map/deliver/pallas_call | solution.py:590
  102.4 0.8 reduce
  103.2 0.1 reshape_squeeze.3
  103.4 0.7 reshape.123
  104.1 1.7 %copy.27 = f32[16,4096]{1,0:T(8,128)} copy(f32[16,4096]{1,0:T(8,128)} %get-tuple-element.26) | data formatting | bytes 524288
  (8 shorter events, 0.1 us)
Async XLA Ops:
  2.4 1.2 %copy-start = (f32[4,16,4096]{2,1,0:T(8,128)S(1)}, f32[4,16,4096]{2,1,0:T(8,128)}, u32[]{:S(2)}) copy-start(f32[4,16,4096]{2,1,0:T(8,128)} %start_ref.1) | copy-start | bytes 3145732
  3.7 0.7 copy-start.2
  90.5 0.7 copy-start.1

commit v5 on v4

--- a/solution.py
+++ b/solution.py
@@ -21,11 +21,12 @@
 LANES = 128
 SUBS = 8
 GROUP = 8
-EDGE = 4
+EDGE = 8
 UNROLL = 32
 VMEM = pl.BlockSpec(memory_space=pltpu.VMEM)
 SMEM = pl.BlockSpec(memory_space=pltpu.SMEM)
 ANY = pl.BlockSpec(memory_space=pl.ANY)
+HBM = pl.BlockSpec(memory_space=pltpu.HBM)
 PARAMS = pltpu.CompilerParams(vmem_limit_bytes=48 * 1024 * 1024)
 MESH = pl.DeviceIdType.MESH
 
@@ -505,7 +506,7 @@
             jax.ShapeDtypeStruct((high * phases * SUBS, LANES), f32),
             jax.ShapeDtypeStruct((SLAB,) + info.shape, jnp.int32),
         ),
-        in_specs=[SMEM, SMEM, ANY, ANY, ANY],
+        in_specs=[SMEM, SMEM, HBM, ANY, ANY],
         out_specs=(VMEM, VMEM, ANY),
         scratch_shapes=[
             pltpu.VMEM((half, half), f32),

time: 106 us -> 104 us (0.981)
  Pallas kernels: 95.7 us -> 93.8 us
    pallas_call x1, Pallas kernels: 55.3 us -> 53.5 us  [on_device(): pl.pallas_call(functools.partial(march, count), out_shape=jax.ShapeDtypeS...]
where the time goes in v5:
time: 104 us
  Pallas kernels  93.8 us (90%)
  local copies, waits for them, and re-layouts  6.02 us (6%)
  other arithmetic  2.91 us (3%)
    pallas_call x1, Pallas kernels, on_device(): pl.pallas_call(functools.partial(march, count), out_shape=jax.ShapeDtypeS...  53.5 us
    pallas_call x1, Pallas kernels, on_device(): pl.pallas_call(functools.partial(gather, count), out_shape=(jax.ShapeDtyp...  26.1 us
    pallas_call x1, Pallas kernels, on_device(): pl.pallas_call(functools.partial(deliver, count, size), out_shape=(jax.Sh...  9.85 us
    pallas_call x1, Pallas kernels, on_device(): pl.pallas_call(finish, out_shape=(jax.ShapeDtypeStruct((SLAB, rows, windo...  4.41 us
    unnamed x7, local copies, waits for them, and re-layouts  4.26 us

profile of v5, /device:TPU:0, one launch (start us, length us, event | category | flops | bytes accessed | tf_op | source)
XLA Modules:
  0.0 103.9 jit_solution(176513213160083321)
XLA Ops:
  0.7 1.1 %compare_select_fusion.cost_ref = f32[16,4096]{1,0:T(8,128)S(1)} fusion(f32[16,4096]{1,0:T(8,128)} %param.6, s32[16,4096]{1,0:T(8,128)} %param.7), kind=kLoop, calls=%fused_computation.4 | loop fusion | flops 131072 | bytes 786432 | tf_op jit(solution)/shard_map/jit(_where)/select_n | solution.py:497
  1.8 0.7 pad_add_fusion
  2.4 0.0 copy-start
  2.4 1.2 %copy-done = f32[4,16,4096]{2,1,0:T(8,128)S(1)} copy-done((f32[4,16,4096]{2,1,0:T(8,128)S(1)}, f32[4,16,4096]{2,1,0:T(8,128)}, u32[]{:S(2)}) %copy-start) | copy-done | bytes 1048600
  3.7 0.0 copy-start.2
  3.7 0.7 copy-done.2
  4.3 26.1 %gather.1 = (f32[2560,128]{1,0:T(8,128)S(1)}, f32[3840,128]{1,0:T(8,128)S(1)}, s32[4,2,1,128]{3,2,1,0:T(1,128)S(1)}) custom-call(s32[1]{0:T(128)} %bitcast.1.first_ref, s32[4]{0:T(128)S(1)} %copy-done.2, f32[4,16,4096]{2,1,0:T(8,128)S(1)} %copy-done, f32[16,4096]{1,0:T(8,128)S(1)} %compare_select_fusion.cost_ref, s32[2,1,128]{2,1,0:T(1,128)S(1)} %bitcast.33), custom_call_target="tpu_custom_call" | custom-call | tf_op jit(solution)/shard_map/gather/pallas_call | solution.py:502
  30.4 0.2 convert_reduce_fusion
  30.7 53.5 %march.1 = f32[64,5,8,128]{3,2,1,0:T(8,128)S(1)} custom-call(f32[64,5,8,128]{3,2,1,0:T(8,128)S(1)} %bitcast.31, f32[96,5,8,128]{3,2,1,0:T(8,128)S(1)} %bitcast.30), custom_call_target="tpu_custom_call" | custom-call | tf_op jit(solution)/shard_map/march/pallas_call | solution.py:527
  84.2 0.1 add_select_fusion.3
  84.2 4.4 %finish.1 = (f32[4,16,1280]{2,1,0:T(8,128)S(1)}, f32[4,8,128]{2,1,0:T(8,128)S(1)}) custom-call(s32[512]{0:T(512)S(1)} %get-tuple-element.23.spots_ref, s32[512]{0:T(512)S(1)} %get-tuple-element.22.turns_ref, f32[2560,128]{1,0:T(8,128)S(1)} %bitcast.29), custom_call_target="tpu_custom_call" | custom-call | tf_op jit(solution)/shard_map/finish/pallas_call | solution.py:555
  88.6 0.0 copy-start.1
  88.7 0.7 copy-done.1
  89.4 0.3 fusion
  89.7 0.1 reshape.121
  89.9 0.1 copy.25
  89.9 0.7 reshape.122.send_ref
  90.7 9.8 %deliver.1 = (f32[16,4096]{1,0:T(8,128)}, f32[16,1,256]{2,1,0:T(1,128)}) custom-call(f32[4,16,1280]{2,1,0:T(8,128)} %copy-done.1, f32[16,1,256]{2,1,0:T(1,128)} %reshape.122.send_ref), custom_call_target="tpu_custom_call" | custom-call | tf_op jit(solution)/shard_map/deliver/pallas_call | solution.py:591
  100.5 0.8 reduce
  101.3 0.1 reshape_squeeze.3
  101.5 0.7 reshape.123
  102.2 1.7 %copy.27 = f32[16,4096]{1,0:T(8,128)} copy(f32[16,4096]{1,0:T(8,128)} %get-tuple-element.26) | data formatting | bytes 524288
  (8 shorter events, 0.1 us)
Async XLA Ops:
  2.4 1.2 %copy-start = (f32[4,16,4096]{2,1,0:T(8,128)S(1)}, f32[4,16,4096]{2,1,0:T(8,128)}, u32[]{:S(2)}) copy-start(f32[4,16,4096]{2,1,0:T(8,128)} %start_ref.1) | copy-start | bytes 3145732
  3.7 0.7 copy-start.2
  88.6 0.7 copy-start.1
